TPU v7x, 128 devices: a whole 4x4x4 slice. The times are simulated.
128 devices in a mesh: tm: 8 (over z, core), height: 16 (over x, y).
Axes of the slice: x: 4, y: 4, z: 4, core: 2. Of those that a mesh axis runs over, the one named last changes fastest.
Arguments:
- tokens: bfloat16 [16, 32, 64, 1536], P('tm', 'height'), may hold values from -6 to 6
- norm_gain: float32 [1536], replicated, may hold values from 0.5 to 1.5
- in_weight: bfloat16 [1536, 3072], replicated, may hold values from -0.15625 to 0.15625
- bc_weight: bfloat16 [1536, 512], replicated, may hold values from -0.15625 to 0.15625
- dt_weight: bfloat16 [1536, 48], replicated, may hold values from -0.15625 to 0.15625
- dt_bias: float32 [48], replicated, may hold values from -1 to 1
- decay_rate: float32 [2, 24], replicated, may hold values from 0.00032552084 to 0.05
- out_gain: float32 [1536], replicated, may hold values from 0.5 to 1.5
- out_weight: bfloat16 [1536, 1536], replicated, may hold values from -0.15625 to 0.15625
Outputs:
- mixed: bfloat16 [16, 32, 64, 1536], P('tm', 'height')
All inputs are finite; a program needn't handle non-finite values.
Results may differ from a plain program's by a relative error of at most 0.02.
Values may be sent and summed in bfloat16 or wider, within the bound.
A program may use at most 192 MiB of HBM per device.

v0:
```python
import math

import jax
import jax.numpy as jnp
from jax import lax
from jax.sharding import PartitionSpec as P

PRECISE = lax.Precision.HIGH
EPSILON = 1e-05


def passed_along(value, axis, steps):
    count = lax.axis_size(axis)
    initial, last = (max(0, -steps), min(count, count - steps))
    return lax.ppermute(value, axis, [(source, source + steps) for source in range(initial, last)])


def carried_in(value, axis, combine, identity):
    count, here = (lax.axis_size(axis), lax.axis_index(axis))
    everything = jax.tree.map(
        lambda part, kind: lax.all_gather(part.astype(kind), axis),
        value,
        (jnp.bfloat16, jnp.bfloat16),
    )
    start = jax.tree.map(
        lambda part, zero: jnp.broadcast_to(jnp.asarray(zero, part.dtype), part.shape),
        value,
        identity,
    )

    def step(k, before):
        reached = k < here
        new = combine(
            before, jax.tree.map(lambda part, own: part[k].astype(own.dtype), everything, value)
        )
        return jax.tree.map(lambda a, b: jnp.where(reached, a, b), new, before)

    return lax.fori_loop(0, count, step, start)


def stored(values):
    return lax.optimization_barrier(values.astype(jnp.bfloat16))


def rms_scale(values, scaling):
    mean_square = jnp.mean(values * values, axis=-1, keepdims=True)
    return values * lax.rsqrt(mean_square + EPSILON) * scaling


def project(left, right):
    return jnp.dot(left, right, preferred_element_type=jnp.float32)


def block_step(carried, pieces):
    inputs, b_proj, c_proj, dt_values, log_decay = pieces
    running = jnp.cumsum(log_decay, axis=0)
    length = inputs.shape[0]
    causal = jnp.arange(length)[:, None] >= jnp.arange(length)[None, :]
    spread = running[:, None, :] - running[None, :, :]
    decays = jnp.exp(jnp.where(causal[:, :, None], spread, -jnp.inf))
    scores = jnp.dot(
        c_proj.astype(jnp.bfloat16),
        b_proj.astype(jnp.bfloat16).T,
        preferred_element_type=jnp.float32,
    )
    weights = scores[:, :, None] * decays * dt_values[None, :, :]
    within = jnp.einsum("ijh,jhp->ihp", weights, inputs, precision=PRECISE)
    earlier = jnp.einsum("in,hpn->ihp", c_proj, carried, precision=PRECISE)
    outputs = within + jnp.exp(running)[:, :, None] * earlier
    to_end = jnp.exp(running[-1][None, :] - running) * dt_values
    fresh_state = jnp.einsum("jh,jhp,jn->hpn", to_end, inputs, b_proj, precision=PRECISE)
    carried = jnp.exp(running[-1])[:, None, None] * carried + fresh_state
    return (carried, outputs)


def run_blocks(inputs, b_proj, c_proj, dt_values, log_decay, initial, block_len):
    blocks = inputs.shape[0] // block_len

    def split_blocks(operand):
        return operand.reshape((blocks, block_len) + operand.shape[1:])

    final_state, outputs = lax.scan(
        block_step,
        initial,
        (
            split_blocks(inputs),
            split_blocks(b_proj),
            split_blocks(c_proj),
            split_blocks(dt_values),
            split_blocks(log_decay),
        ),
    )
    return (outputs.reshape(inputs.shape), final_state)


def local_scan(inputs, b_proj, c_proj, dt_values, log_decay):
    length = inputs.shape[1]
    block_len = math.gcd(256, length)
    initial = jnp.zeros((inputs.shape[2], inputs.shape[3], b_proj.shape[2]), jnp.float32)

    def single(inputs_one, b_one, c_one, dt_one, decay_one):
        return run_blocks(inputs_one, b_one, c_one, dt_one, decay_one, initial, block_len)

    outputs, local_state = jax.vmap(single)(inputs, b_proj, c_proj, dt_values, log_decay)
    running = jnp.cumsum(log_decay, axis=1)
    return (outputs, local_state, running)


def add_incoming(outputs, c_proj, running, incoming):
    earlier = jnp.einsum("bln,bhpn->blhp", c_proj, incoming, precision=PRECISE)
    return outputs + jnp.exp(running)[..., None] * earlier


def link(earlier, later):
    return (earlier[0] * later[0], later[0][..., None, None] * earlier[1] + later[1])


def per_device(
    tokens, norm_gain, in_weight, bc_weight, dt_weight, dt_bias, decay_rate, out_gain, out_weight
):
    frames_dev, rows_dev, columns, model_width = tokens.shape
    heads = decay_rate.shape[1]
    inner = out_weight.shape[0]
    head_dim = inner // heads
    state_dim = bc_weight.shape[1] // 4
    tm_count = lax.axis_size("tm")
    col_block = columns // tm_count
    all_frames = frames_dev * tm_count
    grid_dev = (frames_dev, rows_dev, columns)
    normed = stored(rms_scale(tokens.reshape(-1, model_width).astype(jnp.float32), norm_gain))
    projected = stored(project(normed, in_weight))
    bc_values = stored(project(normed, bc_weight))
    dt_logits = stored(project(normed, dt_weight))
    tm_inputs, tm_bc, tm_logits = (
        lax.all_to_all(
            projected[:, :inner].reshape(grid_dev + (inner,)),
            "tm",
            split_axis=2,
            concat_axis=0,
            tiled=True,
        ),
        lax.all_to_all(
            bc_values[:, 2 * state_dim :].reshape(grid_dev + (2 * state_dim,)),
            "tm",
            split_axis=2,
            concat_axis=0,
            tiled=True,
        ),
        lax.all_to_all(
            dt_logits[:, heads:].reshape(grid_dev + (heads,)),
            "tm",
            split_axis=2,
            concat_axis=0,
            tiled=True,
        ),
    )
    spatial_len = rows_dev * columns
    sp_inputs = (
        projected[:, :inner].astype(jnp.float32).reshape(frames_dev, spatial_len, heads, head_dim)
    )
    sp_bc = (
        bc_values[:, : 2 * state_dim]
        .astype(jnp.float32)
        .reshape(frames_dev, spatial_len, 2 * state_dim)
    )
    sp_dt = jax.nn.softplus(dt_logits[:, :heads].astype(jnp.float32) + dt_bias[:heads]).reshape(
        frames_dev, spatial_len, heads
    )
    sp_decay = -sp_dt * decay_rate[0]
    sp_out, sp_local, sp_running = local_scan(
        sp_inputs, sp_bc[..., :state_dim], sp_bc[..., state_dim:], sp_dt, sp_decay
    )
    sp_total = jnp.exp(sp_running[:, -1])

    def relay(position, incoming):
        return passed_along(
            (sp_total[..., None, None] * incoming + sp_local).astype(jnp.bfloat16), "height", 1
        ).astype(jnp.float32)

    sp_incoming = lax.fori_loop(0, lax.axis_size("height") - 1, relay, jnp.zeros_like(sp_local))
    sp_out = add_incoming(sp_out, sp_bc[..., state_dim:], sp_running, sp_incoming)
    tm_len = col_block * all_frames

    def row_order(operand):
        moved = jnp.transpose(operand, (1, 2, 0, 3))
        return moved.reshape(rows_dev, tm_len, operand.shape[3])

    tm_values = row_order(tm_inputs).astype(jnp.float32).reshape(rows_dev, tm_len, heads, head_dim)
    tm_bcf = row_order(tm_bc).astype(jnp.float32)
    tm_dt = jax.nn.softplus(row_order(tm_logits).astype(jnp.float32) + dt_bias[heads:])
    tm_decay = -tm_dt * decay_rate[1]
    tm_out, tm_local, tm_running = local_scan(
        tm_values, tm_bcf[..., :state_dim], tm_bcf[..., state_dim:], tm_dt, tm_decay
    )
    tm_total = jnp.exp(tm_running[:, -1])
    _, tm_incoming = carried_in(
        (tm_total, tm_local), "tm", link, (jnp.ones_like(tm_total), jnp.zeros_like(tm_local))
    )
    tm_out = add_incoming(tm_out, tm_bcf[..., state_dim:], tm_running, tm_incoming)
    tm_out = stored(
        jnp.transpose(tm_out.reshape(rows_dev, col_block, all_frames, inner), (2, 0, 1, 3))
    )
    returned = lax.all_to_all(tm_out, "tm", split_axis=0, concat_axis=2, tiled=True)
    gate_values = projected[:, inner:].astype(jnp.float32)
    combined = sp_out.reshape(-1, inner) + returned.reshape(-1, inner).astype(jnp.float32)
    gated = combined * jax.nn.silu(gate_values)
    normed_out = stored(rms_scale(gated, out_gain))
    mixed = project(normed_out, out_weight)
    return mixed.astype(jnp.bfloat16).reshape(frames_dev, rows_dev, columns, model_width)


def solution(mesh):
    in_specs = (P("tm", "height", None, None), P(), P(), P(), P(), P(), P(), P(), P())
    out_specs = P("tm", "height", None, None)
    return jax.shard_map(
        per_device, mesh=mesh, in_specs=in_specs, out_specs=out_specs, check_vma=False
    )
```

profile of v0, /device:TPU:2, one launch (start us, length us, event | category | flops | bytes accessed | tf_op | source)
XLA Modules:
  0.0 497.8 jit_solution(8882349971203809938)
XLA Ops:
  10.8 5.3 %all-to-all-start.2 = ((bf16[8,2,384]{2,1,0:T(2,128)(2,1)}), bf16[8,2,384]{2,1,0:T(2,128)(2,1)S(1)}, u32[]{:S(2)}, u32[]{:S(2)}) async-start(bf16[8,2,384]{2,1,0:T(2,128)(2,1)} %reshape.201), calls=%async_computation.2 | async-start | bytes 24576 | tf_op jit(solution)/shard_map/all_to_all | solution.py:149
  16.9 7.4 %convolution_convert_fusion = bf16[256,3072]{1,0:T(8,128)(2,1)} fusion(bf16[256,1536]{1,0:T(8,128)(2,1)S(1)} %fusion.25, bf16[1536,3072]{1,0:T(8,128)(2,1)} %param.15), kind=kOutput, calls=%fused_computation.6 | convolution fusion | flops 2416705536 | bytes 11796480 | tf_op jit(solution)/shard_map/dot_general | solution.py:51
  28.8 4.8 all-to-all-start.1
  33.9 5.9 %all-to-all-done.1 = bf16[2,2,64,256]{3,1,0,2:T(2,128)(2,1)S(1)} async-done(((bf16[2,2,64,256]{3,1,0,2:T(2,128)(2,1)}), bf16[2,2,64,256]{3,1,0,2:T(2,128)(2,1)S(1)}, u32[]{:S(2)}, u32[]{:S(2)}) %all-to-all-start.1) | async-done | bytes 131104 | tf_op jit(solution)/shard_map/all_to_all | solution.py:142
  39.8 3.5 all-to-all-start
  45.9 10.5 %all-to-all-done = bf16[2,2,64,1536]{3,1,0,2:T(2,128)(2,1)S(1)} async-done(((bf16[2,2,64,1536]{3,1,0,2:T(2,128)(2,1)}), bf16[2,2,64,1536]{3,1,0,2:T(2,128)(2,1)S(1)}, u32[]{:S(2)}, u32[]{:S(2)}) %all-to-all-start) | async-done | bytes 786464 | tf_op jit(solution)/shard_map/all_to_all | solution.py:135
  58.0 2.4 squeeze.47
  61.5 2.7 add_convert_fusion
  68.7 9.1 %all-gather = bf16[16,1,24]{2,1,0:T(2,128)(2,1)S(1)} all-gather(bf16[2,1,24]{2,1,0:T(2,128)(2,1)S(1)} %copy-done.15), channel_id=2, replica_groups=mesh['tm'=8,'height'=16] {'tm'}, dimensions={0}, use_global_device_ids=true | all-gather | bytes 864 | tf_op jit(solution)/shard_map/all_gather | solution.py:21
  78.8 3.4 fusion.11
  84.8 4.0 fusion.5
  88.8 16.3 %all-gather.4.cloned.1.call-done = bf16[16,24,64,128]{3,2,1,0:T(8,128)(2,1)} async-done(((bf16[2,24,64,128]{3,2,1,0:T(8,128)(2,1)}), bf16[16,24,64,128]{3,2,1,0:T(8,128)(2,1)}) %all-gather.4.cloned.1.call-update) | async-done | bytes 6291472 | tf_op jit(solution)/shard_map/all_gather | solution.py:21
  105.1 24.3 %while.17 = (s32[]{:T(128)}, f32[2,24,64,128]{3,2,1,0:T(8,128)}, s32[]{:T(128)}, bf16[8,2,24]{2,1,0:T(2,128)(2,1)S(1)}, bf16[8,2,24,64,128]{4,3,2,1,0:T(8,128)(2,1)}, /*index=5*/s32[]{:T(128)}, s32[]{:T(128)}) while((s32[]{:T(128)}, f32[2,24,64,128]{3,2,1,0:T(8,128)}, s32[]{:T(128)}, bf16[8,2,24]{2,1,0:T(2,128)(2,1)S(1)}, ...), condition=%wide.region_6.7_spmd.clone, body=%wide.region_5.6_spmd.clone.sunk | while | flops 1966132 | bytes 3932745 | solution.py:38
  105.1 2.6 fusion.93
  107.7 3.1 fusion.93
  110.8 3.1 fusion.93
  113.9 3.1 fusion.93
  117.0 3.1 fusion.93
  120.1 3.1 fusion.93
  123.2 3.1 fusion.93
  126.2 3.1 fusion.93
  129.3 4.0 fusion.22
  133.3 2.7 copy.103
  136.0 3.4 convert_element_type.148
  139.4 2.5 copy.104
  141.8 4.2 all-to-all-start.3
  146.1 328.8 %while.16 = (s32[]{:T(128)}, f32[2,24,64,128]{3,2,1,0:T(8,128)S(1)}, f32[2,24]{1,0:T(2,128)S(1)}, f32[2,24,64,128]{3,2,1,0:T(8,128)S(1)}, s32[]{:T(128)}, /*index=5*/s32[]{:T(128)}) while((s32[]{:T(128)}, f32[2,24,64,128]{3,2,1,0:T(8,128)S(1)}, f32[2,24]{1,0:T(2,128)S(1)}, f32[2,24,64,128]{3,2,1,0:T(8,128)S(1)}, s32[]{:T(128)}, ...), condition=%wide.region_3.4_spmd.clone, body=%wide.region_2.3_spmd.clone.sunk | while | flops 1966083 | bytes 9437495 | solution.py:180
  147.2 3.4 collective-permute-start
  150.6 20.7 %collective-permute-done = bf16[2,24,64,128]{3,2,1,0:T(8,128)(2,1)} collective-permute-done((bf16[2,24,64,128]{3,2,1,0:T(8,128)(2,1)}, bf16[2,24,64,128]{3,2,1,0:T(8,128)(2,1)}, u32[]{:S(2)}, u32[]{:S(2)}) %collective-permute-start) | collective-permute-done | bytes 786464 | tf_op jit(solution)/shard_map/while/body/eval_jaxpr/ppermute | solution.py:15
  173.8 1.9 collective-permute-start
  175.7 21.4 %collective-permute-done = bf16[2,24,64,128]{3,2,1,0:T(8,128)(2,1)} collective-permute-done((bf16[2,24,64,128]{3,2,1,0:T(8,128)(2,1)}, bf16[2,24,64,128]{3,2,1,0:T(8,128)(2,1)}, u32[]{:S(2)}, u32[]{:S(2)}) %collective-permute-start) | collective-permute-done | bytes 786464 | tf_op jit(solution)/shard_map/while/body/eval_jaxpr/ppermute | solution.py:15
  201.5 20.5 %collective-permute-done = bf16[2,24,64,128]{3,2,1,0:T(8,128)(2,1)} collective-permute-done((bf16[2,24,64,128]{3,2,1,0:T(8,128)(2,1)}, bf16[2,24,64,128]{3,2,1,0:T(8,128)(2,1)}, u32[]{:S(2)}, u32[]{:S(2)}) %collective-permute-start) | collective-permute-done | bytes 786464 | tf_op jit(solution)/shard_map/while/body/eval_jaxpr/ppermute | solution.py:15
  226.4 19.5 %collective-permute-done = bf16[2,24,64,128]{3,2,1,0:T(8,128)(2,1)} collective-permute-done((bf16[2,24,64,128]{3,2,1,0:T(8,128)(2,1)}, bf16[2,24,64,128]{3,2,1,0:T(8,128)(2,1)}, u32[]{:S(2)}, u32[]{:S(2)}) %collective-permute-start) | collective-permute-done | bytes 786464 | tf_op jit(solution)/shard_map/while/body/eval_jaxpr/ppermute | solution.py:15
  250.3 18.6 %collective-permute-done = bf16[2,24,64,128]{3,2,1,0:T(8,128)(2,1)} collective-permute-done((bf16[2,24,64,128]{3,2,1,0:T(8,128)(2,1)}, bf16[2,24,64,128]{3,2,1,0:T(8,128)(2,1)}, u32[]{:S(2)}, u32[]{:S(2)}) %collective-permute-start) | collective-permute-done | bytes 786464 | tf_op jit(solution)/shard_map/while/body/eval_jaxpr/ppermute | solution.py:15
  273.3 17.7 %collective-permute-done = bf16[2,24,64,128]{3,2,1,0:T(8,128)(2,1)} collective-permute-done((bf16[2,24,64,128]{3,2,1,0:T(8,128)(2,1)}, bf16[2,24,64,128]{3,2,1,0:T(8,128)(2,1)}, u32[]{:S(2)}, u32[]{:S(2)}) %collective-permute-start) | collective-permute-done | bytes 786464 | tf_op jit(solution)/shard_map/while/body/eval_jaxpr/ppermute | solution.py:15
  295.4 16.8 %collective-permute-done = bf16[2,24,64,128]{3,2,1,0:T(8,128)(2,1)} collective-permute-done((bf16[2,24,64,128]{3,2,1,0:T(8,128)(2,1)}, bf16[2,24,64,128]{3,2,1,0:T(8,128)(2,1)}, u32[]{:S(2)}, u32[]{:S(2)}) %collective-permute-start) | collective-permute-done | bytes 786464 | tf_op jit(solution)/shard_map/while/body/eval_jaxpr/ppermute | solution.py:15
  316.6 15.9 %collective-permute-done = bf16[2,24,64,128]{3,2,1,0:T(8,128)(2,1)} collective-permute-done((bf16[2,24,64,128]{3,2,1,0:T(8,128)(2,1)}, bf16[2,24,64,128]{3,2,1,0:T(8,128)(2,1)}, u32[]{:S(2)}, u32[]{:S(2)}) %collective-permute-start) | collective-permute-done | bytes 786464 | tf_op jit(solution)/shard_map/while/body/eval_jaxpr/ppermute | solution.py:15
  336.8 14.9 %collective-permute-done = bf16[2,24,64,128]{3,2,1,0:T(8,128)(2,1)} collective-permute-done((bf16[2,24,64,128]{3,2,1,0:T(8,128)(2,1)}, bf16[2,24,64,128]{3,2,1,0:T(8,128)(2,1)}, u32[]{:S(2)}, u32[]{:S(2)}) %collective-permute-start) | collective-permute-done | bytes 786464 | tf_op jit(solution)/shard_map/while/body/eval_jaxpr/ppermute | solution.py:15
  356.1 14.4 %collective-permute-done = bf16[2,24,64,128]{3,2,1,0:T(8,128)(2,1)} collective-permute-done((bf16[2,24,64,128]{3,2,1,0:T(8,128)(2,1)}, bf16[2,24,64,128]{3,2,1,0:T(8,128)(2,1)}, u32[]{:S(2)}, u32[]{:S(2)}) %collective-permute-start) | collective-permute-done | bytes 786464 | tf_op jit(solution)/shard_map/while/body/eval_jaxpr/ppermute | solution.py:15
  374.9 15.1 %collective-permute-done = bf16[2,24,64,128]{3,2,1,0:T(8,128)(2,1)} collective-permute-done((bf16[2,24,64,128]{3,2,1,0:T(8,128)(2,1)}, bf16[2,24,64,128]{3,2,1,0:T(8,128)(2,1)}, u32[]{:S(2)}, u32[]{:S(2)}) %collective-permute-start) | collective-permute-done | bytes 786464 | tf_op jit(solution)/shard_map/while/body/eval_jaxpr/ppermute | solution.py:15
  394.4 16.1 %collective-permute-done = bf16[2,24,64,128]{3,2,1,0:T(8,128)(2,1)} collective-permute-done((bf16[2,24,64,128]{3,2,1,0:T(8,128)(2,1)}, bf16[2,24,64,128]{3,2,1,0:T(8,128)(2,1)}, u32[]{:S(2)}, u32[]{:S(2)}) %collective-permute-start) | collective-permute-done | bytes 786464 | tf_op jit(solution)/shard_map/while/body/eval_jaxpr/ppermute | solution.py:15
  414.9 17.2 %collective-permute-done = bf16[2,24,64,128]{3,2,1,0:T(8,128)(2,1)} collective-permute-done((bf16[2,24,64,128]{3,2,1,0:T(8,128)(2,1)}, bf16[2,24,64,128]{3,2,1,0:T(8,128)(2,1)}, u32[]{:S(2)}, u32[]{:S(2)}) %collective-permute-start) | collective-permute-done | bytes 786464 | tf_op jit(solution)/shard_map/while/body/eval_jaxpr/ppermute | solution.py:15
  436.5 18.3 %collective-permute-done = bf16[2,24,64,128]{3,2,1,0:T(8,128)(2,1)} collective-permute-done((bf16[2,24,64,128]{3,2,1,0:T(8,128)(2,1)}, bf16[2,24,64,128]{3,2,1,0:T(8,128)(2,1)}, u32[]{:S(2)}, u32[]{:S(2)}) %collective-permute-start) | collective-permute-done | bytes 786464 | tf_op jit(solution)/shard_map/while/body/eval_jaxpr/ppermute | solution.py:15
  459.2 14.4 %collective-permute-done = bf16[2,24,64,128]{3,2,1,0:T(8,128)(2,1)} collective-permute-done((bf16[2,24,64,128]{3,2,1,0:T(8,128)(2,1)}, bf16[2,24,64,128]{3,2,1,0:T(8,128)(2,1)}, u32[]{:S(2)}, u32[]{:S(2)}) %collective-permute-start) | collective-permute-done | bytes 786464 | tf_op jit(solution)/shard_map/while/body/eval_jaxpr/ppermute | solution.py:15
  474.9 2.6 fusion.23
  477.5 2.2 copy.111
  479.7 2.8 reshape.200
  486.2 4.7 convolution_convert_fusion.1
  (152 shorter events, 87.8 us)
Async XLA Ops:
  6.5 17.8 %copy-start = (bf16[1536,512]{1,0:T(8,128)(2,1)S(1)}, bf16[1536,512]{1,0:T(8,128)(2,1)}, u32[]{:S(2)}) copy-start(bf16[1536,512]{1,0:T(8,128)(2,1)} %param.16) | copy-start | bytes 4718596
  6.5 3.0 copy-start.12
  8.0 8.1 %copy-start.16 = (f32[48]{0:T(128)S(1)}, f32[48]{0:T(128)}, u32[]{:S(2)}) copy-start(f32[48]{0:T(128)} %param.18) | copy-start | bytes 580
  10.8 18.0 %all-to-all-start.2 = ((bf16[8,2,384]{2,1,0:T(2,128)(2,1)}), bf16[8,2,384]{2,1,0:T(2,128)(2,1)S(1)}, u32[]{:S(2)}, u32[]{:S(2)}) async-start(bf16[8,2,384]{2,1,0:T(2,128)(2,1)} %reshape.201), calls=%async_computation.2 | async-start | bytes 24576 | tf_op jit(solution)/shard_map/all_to_all | solution.py:149
  24.3 0.7 copy-start.17
  25.1 18.3 %copy-start.5 = (f32[256,24]{1,0:T(8,128)}, f32[256,24]{1,0:T(8,128)S(1)}, u32[]{:S(2)}) copy-start(f32[256,24]{1,0:T(8,128)S(1)} %copy.130) | copy-start | bytes 73732
  28.8 10.9 %all-to-all-start.1 = ((bf16[2,2,64,256]{3,1,0,2:T(2,128)(2,1)}), bf16[2,2,64,256]{3,1,0,2:T(2,128)(2,1)S(1)}, u32[]{:S(2)}, u32[]{:S(2)}) async-start(bf16[2,2,64,256]{3,1,0,2:T(2,128)(2,1)} %copy.91), calls=%async_computation.1 | async-start | bytes 262144 | tf_op jit(solution)/shard_map/all_to_all | solution.py:142
  39.8 16.6 %all-to-all-start = ((bf16[2,2,64,1536]{3,1,0,2:T(2,128)(2,1)}), bf16[2,2,64,1536]{3,1,0,2:T(2,128)(2,1)S(1)}, u32[]{:S(2)}, u32[]{:S(2)}) async-start(bf16[2,2,64,1536]{3,1,0,2:T(2,128)(2,1)} %copy.87), calls=%async_computation | async-start | bytes 1572864 | tf_op jit(solution)/shard_map/all_to_all | solution.py:135
  43.3 61.7 %all-gather.4.cloned.1.call-start = ((), (), s32[]{:S(2)}) async-start(), calls=%async_computation.4 | async-start | bytes 7077888 | tf_op jit(solution)/shard_map/all_gather | solution.py:21
  44.1 12.5 %copy-start.7 = (f32[2,128,24]{2,1,0:T(8,128)}, f32[2,128,24]{2,1,0:T(8,128)S(1)}, u32[]{:S(2)}) copy-start(f32[2,128,24]{2,1,0:T(8,128)S(1)} %get-tuple-element.225) | copy-start | bytes 73732
  58.0 2.4 copy-start.9
  60.4 1.2 copy-start.2
  64.8 3.5 copy-start.8
  64.8 3.6 copy-start.10
  64.8 3.9 copy-start.15
  64.8 13.0 %copy-start.11 = (f32[2,128,24]{2,1,0:T(8,128)S(1)}, f32[2,128,24]{2,1,0:T(8,128)}, u32[]{:S(2)}) copy-start(f32[2,128,24]{2,1,0:T(8,128)} %get-tuple-element.228) | copy-start | bytes 73732
  64.8 13.0 %copy-start.6 = (f32[256,24]{1,0:T(8,128)S(1)}, f32[256,24]{1,0:T(8,128)}, u32[]{:S(2)}) copy-start(f32[256,24]{1,0:T(8,128)} %copy-done.5) | copy-start | bytes 73732
  82.9 2.0 copy-start.3
  82.9 2.0 copy-start.13
  141.8 340.7 %all-to-all-start.3 = ((bf16[16,2,8,1536]{3,2,1,0:T(8,128)(2,1)}), bf16[16,2,8,1536]{3,2,1,0:T(8,128)(2,1)}, u32[]{:S(2)}, u32[]{:S(2)}) async-start(bf16[16,2,8,1536]{3,2,1,0:T(8,128)(2,1)} %copy.104), calls=%async_computation.3 | async-start | bytes 1572864 | tf_op jit(solution)/shard_map/all_to_all | solution.py:203
  147.2 24.1 %collective-permute-start = (bf16[2,24,64,128]{3,2,1,0:T(8,128)(2,1)}, bf16[2,24,64,128]{3,2,1,0:T(8,128)(2,1)}, u32[]{:S(2)}, u32[]{:S(2)}) collective-permute-start(bf16[2,24,64,128]{3,2,1,0:T(8,128)(2,1)} %fusion.92), channel_id=1, source_target_pairs={{0,1},{1,2},{2,3},{3,4},{4,5},{5,6},{6,7},{7,8},{8,9},{9,10},{10,1... | collective-permute-start | bytes 2359304 | tf_op jit(solution)/shard_map/while/body/eval_jaxpr/ppermute | solution.py:15
  173.8 23.3 %collective-permute-start = (bf16[2,24,64,128]{3,2,1,0:T(8,128)(2,1)}, bf16[2,24,64,128]{3,2,1,0:T(8,128)(2,1)}, u32[]{:S(2)}, u32[]{:S(2)}) collective-permute-start(bf16[2,24,64,128]{3,2,1,0:T(8,128)(2,1)} %fusion.92), channel_id=1, source_target_pairs={{0,1},{1,2},{2,3},{3,4},{4,5},{5,6},{6,7},{7,8},{8,9},{9,10},{10,1... | collective-permute-start | bytes 2359304 | tf_op jit(solution)/shard_map/while/body/eval_jaxpr/ppermute | solution.py:15
  199.6 22.4 %collective-permute-start = (bf16[2,24,64,128]{3,2,1,0:T(8,128)(2,1)}, bf16[2,24,64,128]{3,2,1,0:T(8,128)(2,1)}, u32[]{:S(2)}, u32[]{:S(2)}) collective-permute-start(bf16[2,24,64,128]{3,2,1,0:T(8,128)(2,1)} %fusion.92), channel_id=1, source_target_pairs={{0,1},{1,2},{2,3},{3,4},{4,5},{5,6},{6,7},{7,8},{8,9},{9,10},{10,1... | collective-permute-start | bytes 2359304 | tf_op jit(solution)/shard_map/while/body/eval_jaxpr/ppermute | solution.py:15
  224.4 21.5 %collective-permute-start = (bf16[2,24,64,128]{3,2,1,0:T(8,128)(2,1)}, bf16[2,24,64,128]{3,2,1,0:T(8,128)(2,1)}, u32[]{:S(2)}, u32[]{:S(2)}) collective-permute-start(bf16[2,24,64,128]{3,2,1,0:T(8,128)(2,1)} %fusion.92), channel_id=1, source_target_pairs={{0,1},{1,2},{2,3},{3,4},{4,5},{5,6},{6,7},{7,8},{8,9},{9,10},{10,1... | collective-permute-start | bytes 2359304 | tf_op jit(solution)/shard_map/while/body/eval_jaxpr/ppermute | solution.py:15
  248.4 20.5 %collective-permute-start = (bf16[2,24,64,128]{3,2,1,0:T(8,128)(2,1)}, bf16[2,24,64,128]{3,2,1,0:T(8,128)(2,1)}, u32[]{:S(2)}, u32[]{:S(2)}) collective-permute-start(bf16[2,24,64,128]{3,2,1,0:T(8,128)(2,1)} %fusion.92), channel_id=1, source_target_pairs={{0,1},{1,2},{2,3},{3,4},{4,5},{5,6},{6,7},{7,8},{8,9},{9,10},{10,1... | collective-permute-start | bytes 2359304 | tf_op jit(solution)/shard_map/while/body/eval_jaxpr/ppermute | solution.py:15
  271.4 19.6 %collective-permute-start = (bf16[2,24,64,128]{3,2,1,0:T(8,128)(2,1)}, bf16[2,24,64,128]{3,2,1,0:T(8,128)(2,1)}, u32[]{:S(2)}, u32[]{:S(2)}) collective-permute-start(bf16[2,24,64,128]{3,2,1,0:T(8,128)(2,1)} %fusion.92), channel_id=1, source_target_pairs={{0,1},{1,2},{2,3},{3,4},{4,5},{5,6},{6,7},{7,8},{8,9},{9,10},{10,1... | collective-permute-start | bytes 2359304 | tf_op jit(solution)/shard_map/while/body/eval_jaxpr/ppermute | solution.py:15
  293.5 18.7 %collective-permute-start = (bf16[2,24,64,128]{3,2,1,0:T(8,128)(2,1)}, bf16[2,24,64,128]{3,2,1,0:T(8,128)(2,1)}, u32[]{:S(2)}, u32[]{:S(2)}) collective-permute-start(bf16[2,24,64,128]{3,2,1,0:T(8,128)(2,1)} %fusion.92), channel_id=1, source_target_pairs={{0,1},{1,2},{2,3},{3,4},{4,5},{5,6},{6,7},{7,8},{8,9},{9,10},{10,1... | collective-permute-start | bytes 2359304 | tf_op jit(solution)/shard_map/while/body/eval_jaxpr/ppermute | solution.py:15
  314.6 17.8 %collective-permute-start = (bf16[2,24,64,128]{3,2,1,0:T(8,128)(2,1)}, bf16[2,24,64,128]{3,2,1,0:T(8,128)(2,1)}, u32[]{:S(2)}, u32[]{:S(2)}) collective-permute-start(bf16[2,24,64,128]{3,2,1,0:T(8,128)(2,1)} %fusion.92), channel_id=1, source_target_pairs={{0,1},{1,2},{2,3},{3,4},{4,5},{5,6},{6,7},{7,8},{8,9},{9,10},{10,1... | collective-permute-start | bytes 2359304 | tf_op jit(solution)/shard_map/while/body/eval_jaxpr/ppermute | solution.py:15
  334.9 16.9 %collective-permute-start = (bf16[2,24,64,128]{3,2,1,0:T(8,128)(2,1)}, bf16[2,24,64,128]{3,2,1,0:T(8,128)(2,1)}, u32[]{:S(2)}, u32[]{:S(2)}) collective-permute-start(bf16[2,24,64,128]{3,2,1,0:T(8,128)(2,1)} %fusion.92), channel_id=1, source_target_pairs={{0,1},{1,2},{2,3},{3,4},{4,5},{5,6},{6,7},{7,8},{8,9},{9,10},{10,1... | collective-permute-start | bytes 2359304 | tf_op jit(solution)/shard_map/while/body/eval_jaxpr/ppermute | solution.py:15
  354.2 16.3 %collective-permute-start = (bf16[2,24,64,128]{3,2,1,0:T(8,128)(2,1)}, bf16[2,24,64,128]{3,2,1,0:T(8,128)(2,1)}, u32[]{:S(2)}, u32[]{:S(2)}) collective-permute-start(bf16[2,24,64,128]{3,2,1,0:T(8,128)(2,1)} %fusion.92), channel_id=1, source_target_pairs={{0,1},{1,2},{2,3},{3,4},{4,5},{5,6},{6,7},{7,8},{8,9},{9,10},{10,1... | collective-permute-start | bytes 2359304 | tf_op jit(solution)/shard_map/while/body/eval_jaxpr/ppermute | solution.py:15
  373.0 17.0 %collective-permute-start = (bf16[2,24,64,128]{3,2,1,0:T(8,128)(2,1)}, bf16[2,24,64,128]{3,2,1,0:T(8,128)(2,1)}, u32[]{:S(2)}, u32[]{:S(2)}) collective-permute-start(bf16[2,24,64,128]{3,2,1,0:T(8,128)(2,1)} %fusion.92), channel_id=1, source_target_pairs={{0,1},{1,2},{2,3},{3,4},{4,5},{5,6},{6,7},{7,8},{8,9},{9,10},{10,1... | collective-permute-start | bytes 2359304 | tf_op jit(solution)/shard_map/while/body/eval_jaxpr/ppermute | solution.py:15
  392.4 18.1 %collective-permute-start = (bf16[2,24,64,128]{3,2,1,0:T(8,128)(2,1)}, bf16[2,24,64,128]{3,2,1,0:T(8,128)(2,1)}, u32[]{:S(2)}, u32[]{:S(2)}) collective-permute-start(bf16[2,24,64,128]{3,2,1,0:T(8,128)(2,1)} %fusion.92), channel_id=1, source_target_pairs={{0,1},{1,2},{2,3},{3,4},{4,5},{5,6},{6,7},{7,8},{8,9},{9,10},{10,1... | collective-permute-start | bytes 2359304 | tf_op jit(solution)/shard_map/while/body/eval_jaxpr/ppermute | solution.py:15
  413.0 19.1 %collective-permute-start = (bf16[2,24,64,128]{3,2,1,0:T(8,128)(2,1)}, bf16[2,24,64,128]{3,2,1,0:T(8,128)(2,1)}, u32[]{:S(2)}, u32[]{:S(2)}) collective-permute-start(bf16[2,24,64,128]{3,2,1,0:T(8,128)(2,1)} %fusion.92), channel_id=1, source_target_pairs={{0,1},{1,2},{2,3},{3,4},{4,5},{5,6},{6,7},{7,8},{8,9},{9,10},{10,1... | collective-permute-start | bytes 2359304 | tf_op jit(solution)/shard_map/while/body/eval_jaxpr/ppermute | solution.py:15
  434.6 20.2 %collective-permute-start = (bf16[2,24,64,128]{3,2,1,0:T(8,128)(2,1)}, bf16[2,24,64,128]{3,2,1,0:T(8,128)(2,1)}, u32[]{:S(2)}, u32[]{:S(2)}) collective-permute-start(bf16[2,24,64,128]{3,2,1,0:T(8,128)(2,1)} %fusion.92), channel_id=1, source_target_pairs={{0,1},{1,2},{2,3},{3,4},{4,5},{5,6},{6,7},{7,8},{8,9},{9,10},{10,1... | collective-permute-start | bytes 2359304 | tf_op jit(solution)/shard_map/while/body/eval_jaxpr/ppermute | solution.py:15
  457.3 16.3 %collective-permute-start = (bf16[2,24,64,128]{3,2,1,0:T(8,128)(2,1)}, bf16[2,24,64,128]{3,2,1,0:T(8,128)(2,1)}, u32[]{:S(2)}, u32[]{:S(2)}) collective-permute-start(bf16[2,24,64,128]{3,2,1,0:T(8,128)(2,1)} %fusion.92), channel_id=1, source_target_pairs={{0,1},{1,2},{2,3},{3,4},{4,5},{5,6},{6,7},{7,8},{8,9},{9,10},{10,1... | collective-permute-start | bytes 2359304 | tf_op jit(solution)/shard_map/while/body/eval_jaxpr/ppermute | solution.py:15
  483.9 1.4 copy-start.4
  485.3 0.7 copy-start.14
  486.2 4.7 copy-start.1
Sparse Core Ops, SparseCore 0:
  64.4 40.5 all-gather.3
where the time goes:
time: 500 us; the launch traced here: 498 us
  waiting for transfers between devices  294 us (59%)
  other arithmetic  70.9 us (14%)
  starting transfers between devices  48.1 us (10%)
  matrix products  34.3 us (7%)
  local copies, waits for them, and re-layouts  26.8 us (5%)
  between operations  13.8 us (3%)
  blocking collectives  9.13 us (2%)
    ppermute x15, waiting for transfers between devices, passed_along(): lax.ppermute(value, axis, [(source, source + steps) for source in range(i...  262 us
    ppermute x15, starting transfers between devices, passed_along(): lax.ppermute(value, axis, [(source, source + steps) for source in range(i...  30.1 us
    select_n x8, other arithmetic, step(): return jax.tree.map(lambda a, b: jnp.where(reached, a, b), new, before)  24.2 us
    convert_element_type x15, other arithmetic, relay(): return passed_along((sp_total[..., None, None] * incoming + sp_local).ast...  19.4 us
    convert_element_type x15, other arithmetic, relay(): (sp_total[..., None, None] * incoming + sp_local).astype(jnp.bfloat16)  17.2 us
    all_gather x1, waiting for transfers between devices, carried_in(): lax.all_gather(part.astype(kind), axis)  16.3 us
    dot_general x4, matrix products, project(): return jnp.dot(left, right, preferred_element_type=jnp.float32)  13 us
    all_to_all x1, waiting for transfers between devices, per_device(): lax.all_to_all(projected[:, :inner].reshape(grid_dev + (inner,)), 'tm', s...  10.5 us
  transfers between devices with their start and end apart: 20, of which 18 were waited for; matrix products, arithmetic and copies ran while one was open for 15% of the time, Pallas kernels for 0%

commit v1 on v0

v1 whole, which is shorter than its diff:
```python
import functools

import jax
import jax.numpy as jnp
from jax import lax
from jax.experimental import pallas as pl
from jax.experimental.pallas import tpu as pltpu
from jax.sharding import PartitionSpec as P

EPSILON = 1e-05
LOG2E = 1.4426950408889634
BF16 = jnp.bfloat16
F32 = jnp.float32

D = 1536
INNER = 1536
HEADS = 24
STATE = 128
COLS = 64
TM = 8
HT = 16
GROUPS = 4
GHEADS = HEADS // GROUPS
GL = GHEADS * 64
TOK = 256
CHUNK_COLS = 16
CHUNKS = COLS // CHUNK_COLS


def mm(a, b):
    return jnp.dot(a, b, preferred_element_type=F32)


def mm_tokens(a, b):
    return lax.dot_general(a, b, (((0,), (0,)), ((), ())), preferred_element_type=F32)


def softplus(v):
    return jnp.maximum(v, 0.0) + jnp.log1p(jnp.exp(-jnp.abs(v)))


def parts(v, count):
    pieces, rest = [], v
    for _ in range(count):
        piece = rest.astype(BF16).astype(F32)
        pieces.append(piece)
        rest = rest - piece
    return jnp.concatenate(pieces, axis=1).astype(BF16)


def cumulative(order, v):
    width = v.shape[1]
    sums = mm(order, parts(v, 3))
    return sums[:, :width] + sums[:, width : 2 * width] + sums[:, 2 * width :]


def iota(shape, dim):
    return lax.broadcasted_iota(jnp.int32, shape, dim)


def kernel(
    tokens, gain, w_in, w_bc, w_dt, dt_bias, rate, out_gain, w_out, out,
    tok_v, w_in_v, w_bc_v, w_dt_v, w_out_v,
    normed, x_all, gate, bc_s, bct_send, l_send, d_send, s_send,
    xt, bct, ltr, d_recv, s_recv, inc_send, inc_recv, y_send, y_recv,
    xd_s, sp_out, e_run, run_s, runt_s, spread_s, spread_t, order_t, lcol, state, d_exp,
    load_sem, x_ssem, x_rsem, b_ssem, b_rsem, l_ssem, l_rsem, d_ssem, d_rsem,
    s_ssem, s_rsem, i_ssem, i_rsem, y_ssem, y_rsem,
):
    t = lax.axis_index("tm")
    h = lax.axis_index("height")
    z = t // 2
    core = t % 2

    def remote(src, dst, ssem, rsem, **where):
        return pltpu.make_async_remote_copy(
            src_ref=src, dst_ref=dst, send_sem=ssem, recv_sem=rsem,
            device_id=where, device_id_type=pl.DeviceIdType.MESH,
        )

    def group_at(step):
        return (z + 1 + step) % GROUPS

    def lanes_of(group):
        return pl.ds(pl.multiple_of(group * GL, 128), GL)

    loads = [
        pltpu.make_async_copy(tokens, tok_v, load_sem.at[0]),
        pltpu.make_async_copy(w_bc, w_bc_v, load_sem.at[1]),
        pltpu.make_async_copy(w_dt, w_dt_v, load_sem.at[2]),
    ]
    for step in range(GROUPS):
        where = lanes_of(group_at(step))
        loads.append(pltpu.make_async_copy(w_in.at[:, where], w_in_v.at[:, where], load_sem.at[3 + step]))
    for step in range(2):
        where = pl.ds(INNER + 768 * step, 768)
        loads.append(pltpu.make_async_copy(w_in.at[:, where], w_in_v.at[:, where], load_sem.at[7 + step]))
    loads.append(pltpu.make_async_copy(w_out, w_out_v, load_sem.at[9]))
    for load in loads:
        load.start()

    barrier = pltpu.get_barrier_semaphore()

    @pl.loop(1, TM)
    def _(k):
        pl.semaphore_signal(barrier, inc=1, device_id={"tm": (t + k) % TM}, device_id_type=pl.DeviceIdType.MESH)

    @pl.loop(1, HT)
    def _(k):
        pl.semaphore_signal(barrier, inc=1, device_id={"height": (h + k) % HT}, device_id_type=pl.DeviceIdType.MESH)

    spread_s[...] = ((iota((96, INNER), 0) & 31) == (iota((96, INNER), 1) >> 6)).astype(F32).astype(BF16)
    spread_t[...] = ((iota((16, GL), 0) & 7) == (iota((16, GL), 1) >> 6)).astype(F32).astype(BF16)

    def place(index):
        return (index & 15) * 16 + ((index >> 4) & 7) * 2 + (index >> 7)

    order_t[...] = (place(iota((TOK, TOK), 0)) >= place(iota((TOK, TOK), 1))).astype(F32).astype(BF16)

    loads[0].wait()

    @pl.loop(0, 8)
    def _(k):
        rows = pl.ds(pl.multiple_of(k * 32, 32), 32)
        v = tok_v[rows, :].astype(F32)
        mean_square = jnp.mean(v * v, axis=-1, keepdims=True)
        normed[rows, :] = (v * lax.rsqrt(mean_square + EPSILON) * gain[...]).astype(BF16)

    loads[1].wait()
    bc = mm(normed[...], w_bc_v[...]).astype(BF16)
    bc_s[...] = bc[:, : 2 * STATE]
    for f in range(2):
        for r in range(2):
            at = 128 * f + 64 * r
            bct_send[r, f] = bc[at : at + 64, 2 * STATE :]
    loads[2].wait()
    logits = mm(normed[...], w_dt_v[...]).astype(BF16).astype(F32)
    dt = softplus(logits + dt_bias[...])
    rates = jnp.concatenate([rate[0:1, :], rate[1:2, :]], axis=1)
    decay = -dt * rates * LOG2E
    both = jnp.concatenate([dt, decay, jnp.zeros((TOK, 32), F32)], axis=1)
    for r in range(2):
        turned = jnp.concatenate([both[64 * r : 64 * r + 64], both[128 + 64 * r : 192 + 64 * r]], axis=0).T
        for g in range(GROUPS):
            l_send[g, r, 0:8] = turned[24 + 6 * g : 32 + 6 * g]
            l_send[g, r, 8:16] = turned[72 + 6 * g : 80 + 6 * g]

    pad = jnp.zeros((TOK, 8), F32)
    dt_s = jnp.concatenate([dt[:, :HEADS], pad], axis=1)
    decay_s = jnp.concatenate([decay[:, :HEADS], pad], axis=1)
    row, col = iota((TOK, TOK), 0), iota((TOK, TOK), 1)
    order_s = ((row >= col) & ((row >> 7) == (col >> 7))).astype(F32).astype(BF16)
    run = cumulative(order_s, decay_s)
    run_s[...] = run
    for f in range(2):
        runt_s[f] = jnp.concatenate([run[128 * f : 128 * f + 128], jnp.zeros((128, 96), F32)], axis=1).T[:32]
    ends = [run[127:128], run[255:256]]
    for f in range(2):
        d_send[f] = jnp.broadcast_to(
            jnp.concatenate([jnp.exp2(ends[f]), jnp.zeros((1, 96), F32)], axis=1), (8, 128)
        )
    end = jnp.concatenate([jnp.broadcast_to(e, (128, 32)) for e in ends], axis=0)
    to_end = parts(jnp.exp2(end - run) * dt_s, 2)
    dt_parts = parts(dt_s, 2)
    from_start = parts(jnp.exp2(run), 2)

    pl.semaphore_wait(barrier, TM - 1 + HT - 1)

    def bc_copy(to):
        return remote(bct_send.at[to % 2], bct.at[t], b_ssem.at[to], b_rsem.at[t], tm=to)

    def l_copy(to):
        return remote(l_send.at[to // 2, to % 2], ltr.at[t], l_ssem.at[to], l_rsem.at[t], tm=to)

    @pl.loop(1, TM)
    def _(k):
        to = (t + k) % TM
        l_copy(to).start()
        bc_copy(to).start()

    bct[t] = bct_send[core]
    ltr[t] = l_send[z, core]

    def owned(p):
        return p // 8, pl.ds(pl.multiple_of((p % 8) * 16, 16), 16)

    def d_copy(to):
        return remote(d_send.at[to // 8], d_recv.at[h], d_ssem.at[to], d_rsem.at[h], height=to)

    @pl.loop(1, HT)
    def _(k):
        d_copy((h + k) % HT).start()

    d_recv[h] = d_send[h // 8]

    def x_source(to):
        rows = pl.ds(pl.multiple_of((to % 2) * COLS, COLS), COLS)
        return x_all.at[:, rows, lanes_of(to // 2)]

    def x_copy(to):
        return remote(x_source(to), xt.at[t], x_ssem.at[to], x_rsem.at[t], tm=to)

    for step in range(GROUPS):
        group = group_at(step)
        loads[3 + step].wait()
        xg = mm(normed[...], w_in_v[:, lanes_of(group)]).astype(BF16)
        x_all[0, :, lanes_of(group)] = xg[:128]
        x_all[1, :, lanes_of(group)] = xg[128:]
        for c in range(2):
            to = group * 2 + c
            if step < GROUPS - 1:
                x_copy(to).start()
            else:
                @pl.when(to != t)
                def _():
                    x_copy(to).start()

                @pl.when(to == t)
                def _():
                    for f in range(2):
                        xt[t, f] = xg[128 * f + COLS * c : 128 * f + COLS * c + COLS]

    for g in range(GROUPS):
        lanes = pl.ds(GL * g, GL)
        spread = spread_s[0:64, lanes]
        weight = mm(to_end, spread)
        steps = mm(dt_parts, spread)
        e_run[:, lanes] = mm(from_start, spread)
        for f in range(2):
            rows = slice(128 * f, 128 * f + 128)
            x = x_all[f, :, lanes].astype(F32)
            xd_s[f, :, lanes] = (x * steps[rows]).astype(BF16)
            s_send[f, :, lanes] = mm_tokens(
                bc_s[rows, :STATE], (x * weight[rows]).astype(BF16)
            ).astype(BF16)

    def s_copy(to):
        f, rows = owned(to)
        return remote(s_send.at[f, rows], s_recv.at[h], s_ssem.at[to], s_rsem.at[h], height=to)

    @pl.loop(1, HT)
    def _(k):
        s_copy((h + k) % HT).start()

    own_f, own_rows = owned(h)
    s_recv[h] = s_send[own_f, own_rows, :]

    for step in range(2):
        loads[7 + step].wait()

        @pl.loop(0, 2)
        def _(k):
            lanes = pl.ds(pl.multiple_of(768 * step + 384 * k, 128), 384)
            source = pl.ds(pl.multiple_of(INNER + 768 * step + 384 * k, 128), 384)
            v = mm(normed[...], w_in_v[:, source]).astype(BF16).astype(F32)
            gate[:, lanes] = v / (1.0 + jnp.exp(-v))

    half = iota((128, 128), 1) < 64
    causal = iota((128, 128), 0) >= iota((128, 128), 1)

    @pl.loop(0, 2)
    def _(f):
        rows = pl.ds(pl.multiple_of(f * 128, 128), 128)
        b, c = bc_s[rows, :STATE], bc_s[rows, STATE:]
        scores = lax.dot_general(c, b, (((1,), (1,)), ((), ())), preferred_element_type=F32)
        scores = jnp.where(causal, scores, 0.0)
        run_f, runt_f = run_s[rows, :], runt_s[f]
        for pair in range(HEADS // 2):
            weights = []
            for head in (2 * pair, 2 * pair + 1):
                spread = run_f[:, head : head + 1] - runt_f[head : head + 1, :]
                weights.append((scores * jnp.exp2(jnp.minimum(spread, 0.0))).astype(BF16))
            lanes = pl.ds(128 * pair, 128)
            x = xd_s[f, :, lanes]
            none = jnp.zeros_like(x)
            both_x = jnp.concatenate([jnp.where(half, x, none), jnp.where(half, none, x)], axis=0)
            sp_out[rows, lanes] = mm(jnp.concatenate(weights, axis=1), both_x)

    @pl.loop(1, HT)
    def _(k):
        source = (h + k) % HT
        remote(d_send.at[0], d_recv.at[source], d_ssem.at[source], d_rsem.at[source], height=source).wait_recv()

    totals = jnp.concatenate([d_recv[k, 0:1, :32] for k in range(HT)], axis=0)
    d_exp[...] = mm(parts(totals, 3), spread_s[...])

    @pl.loop(1, HT)
    def _(k):
        source = (h + k) % HT
        remote(s_send.at[0, pl.ds(0, 16)], s_recv.at[source], s_ssem.at[source], s_rsem.at[source], height=source).wait_recv()

    before = jnp.zeros((16, INNER), F32)
    for k in range(HT):
        inc_send[k] = before.astype(BF16)
        if k < HT - 1:
            before = before * d_exp[k : k + 1, :] + s_recv[k].astype(F32)

    def i_copy(to):
        f, rows = owned(h)
        return remote(inc_send.at[to], inc_recv.at[f, rows], i_ssem.at[to], i_rsem.at[h], height=to)

    @pl.loop(1, HT)
    def _(k):
        i_copy((h + k) % HT).start()

    inc_recv[own_f, own_rows, :] = inc_send[h]

    @pl.loop(1, TM)
    def _(k):
        source = (t + k) % TM
        remote(l_send.at[0, 0], ltr.at[source], l_ssem.at[source], l_rsem.at[source], tm=source).wait_recv()
        remote(bct_send.at[0], bct.at[source], b_ssem.at[source], b_rsem.at[source], tm=source).wait_recv()

    columns = ltr[...].reshape(TM * 16, 128).T
    for s in range(TM):
        lcol[s] = columns[:, 16 * s : 16 * s + 16]

    @pl.loop(1, TM)
    def _(k):
        source = (t + k) % TM
        remote(x_all.at[:, pl.ds(0, COLS), pl.ds(0, GL)], xt.at[source], x_ssem.at[source], x_rsem.at[source], tm=source).wait_recv()

    state[...] = jnp.zeros_like(state)

    def y_copy(to, cols):
        return remote(
            y_send.at[to, :, cols], y_recv.at[t, :, cols], y_ssem.at[to], y_rsem.at[t], tm=to
        )

    @pl.loop(0, CHUNKS)
    def _(chunk):
        cols = pl.ds(pl.multiple_of(chunk * CHUNK_COLS, CHUNK_COLS), CHUNK_COLS)

        def tokens_of(f):
            return pl.ds(pl.multiple_of(f * COLS + chunk * CHUNK_COLS, CHUNK_COLS), CHUNK_COLS)

        def gathered(get, width):
            return jnp.concatenate([get(f).reshape(128, width) for f in range(2)], axis=0)

        x = gathered(lambda f: xt[:, f, cols, :], GL)
        bcv = gathered(lambda f: bct[:, f, cols, :], 2 * STATE)
        dl = gathered(lambda f: lcol[:, tokens_of(f), :], 16)
        b, c = bcv[:, :STATE], bcv[:, STATE:]
        dtv, decays = dl[:, :8], dl[:, 8:]
        runs = cumulative(order_t[...], decays)
        runs_row = jnp.concatenate([runs, jnp.zeros((TOK, 120), F32)], axis=1).T[:8]
        last = runs[TOK - 1 : TOK]
        weight = mm(parts(jnp.exp2(last - runs) * dtv, 2), spread_t[...])
        steps = mm(parts(dtv, 2), spread_t[...])
        grown = mm(parts(jnp.exp2(runs), 2), spread_t[...])
        scores = lax.dot_general(c, b, (((1,), (1,)), ((), ())), preferred_element_type=F32)
        scores = scores * order_t[...].astype(F32)
        xf = x.astype(F32)
        xd = (xf * steps).astype(BF16)
        xw = (xf * weight).astype(BF16)
        earlier = mm(c, state[...].astype(BF16)) * grown
        state[...] = state[...] * grown[TOK - 1 : TOK] + mm_tokens(b, xw)
        half_x = iota((TOK, 128), 1) < 64
        for pair in range(GHEADS // 2):
            weights = []
            for head in (2 * pair, 2 * pair + 1):
                spread = runs[:, head : head + 1] - runs_row[head : head + 1, :]
                weights.append((scores * jnp.exp2(jnp.minimum(spread, 0.0))).astype(BF16))
            lanes = slice(128 * pair, 128 * pair + 128)
            xp = xd[:, lanes]
            none = jnp.zeros_like(xp)
            both_x = jnp.concatenate([jnp.where(half_x, xp, none), jnp.where(half_x, none, xp)], axis=0)
            y = mm(jnp.concatenate(weights, axis=1), both_x) + earlier[:, lanes]
            y = y.astype(BF16)
            for f in range(2):
                y_send[:, f, cols, lanes] = y[128 * f : 128 * f + 128].reshape(TM, CHUNK_COLS, 128)

        @pl.loop(1, TM)
        def _(k):
            y_copy((t + k) % TM, cols).start()

    y_recv[t] = y_send[t]

    @pl.loop(1, HT)
    def _(k):
        source = (h + k) % HT
        f, rows = owned(source)
        remote(inc_send.at[source], inc_recv.at[f, rows], i_ssem.at[source], i_rsem.at[source], height=source).wait_recv()

    for f in range(2):
        rows = slice(128 * f, 128 * f + 128)
        for g in range(GROUPS):
            lanes = slice(GL * g, GL * g + GL)
            sp_out[rows, lanes] += e_run[rows, lanes] * mm(bc_s[rows, STATE:], inc_recv[f, :, lanes])

    @pl.loop(1, TM)
    def _(k):
        source = (t + k) % TM
        remote(y_send.at[source], y_recv.at[source], y_ssem.at[source], y_rsem.at[source], tm=source).wait_recv()

    @pl.loop(0, 8)
    def _(k):
        f, r, part = k // 4, (k // 2) % 2, k % 2
        rows = pl.ds(pl.multiple_of(k * 32, 32), 32)
        cols = pl.ds(pl.multiple_of(part * 32, 32), 32)
        temporal = jnp.concatenate([y_recv[2 * g + r, f, cols, :] for g in range(GROUPS)], axis=1)
        gated = (sp_out[rows, :] + temporal.astype(F32)) * gate[rows, :]
        mean_square = jnp.mean(gated * gated, axis=-1, keepdims=True)
        normed[rows, :] = (gated * lax.rsqrt(mean_square + EPSILON) * out_gain[...]).astype(BF16)

    loads[9].wait()

    @pl.loop(0, 4)
    def _(k):
        lanes = pl.ds(pl.multiple_of(384 * k, 128), 384)
        out[:, lanes] = mm(normed[...], w_out_v[:, lanes]).astype(BF16)

    @pl.loop(1, TM)
    def _(k):
        to = (t + k) % TM
        l_copy(to).wait_send()
        bc_copy(to).wait_send()
        x_copy(to).wait_send()
        y_copy(to, pl.ds(0, COLS)).wait_send()

    @pl.loop(1, HT)
    def _(k):
        to = (h + k) % HT
        d_copy(to).wait_send()
        s_copy(to).wait_send()
        i_copy(to).wait_send()


def per_device(tokens, norm_gain, in_weight, bc_weight, dt_weight, dt_bias, decay_rate, out_gain, out_weight):
    vmem = pl.BlockSpec(memory_space=pltpu.VMEM)
    hbm = pl.BlockSpec(memory_space=pl.ANY)
    dma = pltpu.SemaphoreType.DMA
    out = pl.pallas_call(
        kernel,
        out_shape=jax.ShapeDtypeStruct((TOK, D), BF16),
        in_specs=[hbm, vmem, hbm, hbm, hbm, vmem, vmem, vmem, hbm],
        out_specs=vmem,
        scratch_shapes=[
            pltpu.VMEM((TOK, D), BF16),
            pltpu.VMEM((D, 2 * INNER), BF16),
            pltpu.VMEM((D, 4 * STATE), BF16),
            pltpu.VMEM((D, 2 * HEADS), BF16),
            pltpu.VMEM((INNER, D), BF16),
            pltpu.VMEM((TOK, D), BF16),
            pltpu.VMEM((2, 128, INNER), BF16),
            pltpu.VMEM((TOK, INNER), F32),
            pltpu.VMEM((TOK, 2 * STATE), BF16),
            pltpu.VMEM((2, 2, COLS, 2 * STATE), BF16),
            pltpu.VMEM((GROUPS, 2, 16, 128), F32),
            pltpu.VMEM((2, 8, 128), F32),
            pltpu.VMEM((2, STATE, INNER), BF16),
            pltpu.VMEM((TM, 2, COLS, GL), BF16),
            pltpu.VMEM((TM, 2, COLS, 2 * STATE), BF16),
            pltpu.VMEM((TM, 16, 128), F32),
            pltpu.VMEM((HT, 8, 128), F32),
            pltpu.VMEM((HT, 16, INNER), BF16),
            pltpu.VMEM((HT, 16, INNER), BF16),
            pltpu.VMEM((2, STATE, INNER), BF16),
            pltpu.VMEM((TM, 2, COLS, GL), BF16),
            pltpu.VMEM((TM, 2, COLS, GL), BF16),
            pltpu.VMEM((2, 128, INNER), BF16),
            pltpu.VMEM((TOK, INNER), F32),
            pltpu.VMEM((TOK, INNER), F32),
            pltpu.VMEM((TOK, 32), F32),
            pltpu.VMEM((2, 32, 128), F32),
            pltpu.VMEM((96, INNER), BF16),
            pltpu.VMEM((16, GL), BF16),
            pltpu.VMEM((TOK, TOK), BF16),
            pltpu.VMEM((TM, 128, 16), F32),
            pltpu.VMEM((STATE, GL), F32),
            pltpu.VMEM((HT, INNER), F32),
            dma((10,)),
            dma((TM,)), dma((TM,)), dma((TM,)), dma((TM,)), dma((TM,)), dma((TM,)),
            dma((HT,)), dma((HT,)), dma((HT,)), dma((HT,)), dma((HT,)), dma((HT,)),
            dma((TM,)), dma((TM,)),
        ],
        compiler_params=pltpu.CompilerParams(
            collective_id=0, has_side_effects=True, vmem_limit_bytes=56 * 1024 * 1024
        ),
        name="layer",
    )(
        tokens.reshape(TOK, D),
        norm_gain.reshape(1, D),
        in_weight,
        bc_weight,
        dt_weight,
        dt_bias.reshape(1, 2 * HEADS),
        decay_rate,
        out_gain.reshape(1, INNER),
        out_weight,
    )
    return out.reshape(tokens.shape)


def solution(mesh):
    in_specs = (P("tm", "height", None, None), P(), P(), P(), P(), P(), P(), P(), P())
    out_specs = P("tm", "height", None, None)
    return jax.shard_map(
        per_device, mesh=mesh, in_specs=in_specs, out_specs=out_specs, check_vma=False
    )
```

time: 500 us -> 51.2 us (0.10)
  the two profiles are of different devices: /device:TPU:2 before, /device:TPU:1 now
where the time goes in v1:
time: 51.2 us; the launch traced here: 50.9 us
  Pallas kernels  44.4 us (87%)
  local copies, waits for them, and re-layouts  6.48 us (13%)
    pallas_call x1, Pallas kernels, per_device(): pl.pallas_call(kernel, out_shape=jax.ShapeDtypeStruct((TOK, D), BF16), in...  44.4 us
    unnamed x2, local copies, waits for them, and re-layouts  3.89 us
    reshape x1, local copies, waits for them, and re-layouts, per_device(): out_gain.reshape(1, INNER)  1.3 us
    reshape x1, local copies, waits for them, and re-layouts, per_device(): norm_gain.reshape(1, D)  1.29 us

profile of v1, /device:TPU:1, one launch (start us, length us, event | category | flops | bytes accessed | tf_op | source)
XLA Modules:
  0.0 50.9 jit_solution(10101056180485021628)
XLA Ops:
  0.0 1.3 %reshape.16.gain = f32[1,1536]{1,0:T(1,128)} reshape(f32[1536]{0:T(1024)} %param.10) | data formatting | bytes 12288 | tf_op jit(solution)/shard_map/reshape | solution.py:483
  1.3 1.3 %reshape.18.out_gain = f32[1,1536]{1,0:T(1,128)} reshape(f32[1536]{0:T(1024)} %param.16) | data formatting | bytes 12288 | tf_op jit(solution)/shard_map/reshape | solution.py:489
  2.6 1.8 %copy.10.w_dt = bf16[1536,48]{1,0:T(8,128)(2,1)} copy(bf16[1536,48]{0,1:T(8,128)(2,1)} %param.13) | data formatting | bytes 294912 | tf_op args[4]
  4.4 44.4 %layer.1 = bf16[256,1536]{1,0:T(8,128)(2,1)} custom-call(bf16[256,1536]{1,0:T(8,128)(2,1)} %bitcast.4, f32[1,1536]{1,0:T(1,128)} %reshape.16.gain, bf16[1536,3072]{1,0:T(8,128)(2,1)} %w_in.1, bf16[1536,512]{1,0:T(8,128)(2,1)} %w_bc.1, bf16[1536,48]{1,0:T(8,128)(2,1)} %copy.10.w_dt, f32[1,48]{1,0:T(1,128)} %bitcast.5, f32[2,24]{1,0:T(2,128)} %rate.1, ...), custom_call_target="tpu_custom_call" | custom-call | tf_op jit(solution)/shard_map/layer/pallas_call | solution.py:433
  48.9 2.1 %copy.12 = bf16[2,2,64,1536]{3,2,1,0:T(8,128)(2,1)} copy(bf16[2,2,64,1536]{3,2,1,0:T(8,128)(2,1)} %bitcast.3) | data formatting | bytes 1572864

commit v2 on v1

--- a/solution.py
+++ b/solution.py
@@ -22,6 +22,7 @@
 GROUPS = 4
 GHEADS = HEADS // GROUPS
 GL = GHEADS * 64
+HALF = INNER // 2
 TOK = 256
 CHUNK_COLS = 16
 CHUNKS = COLS // CHUNK_COLS
@@ -33,6 +34,10 @@
 
 def mm_tokens(a, b):
     return lax.dot_general(a, b, (((0,), (0,)), ((), ())), preferred_element_type=F32)
+
+
+def mm_rows(a, b):
+    return lax.dot_general(a, b, (((1,), (1,)), ((), ())), preferred_element_type=F32)
 
 
 def softplus(v):
@@ -64,13 +69,11 @@
     normed, x_all, gate, bc_s, bct_send, l_send, d_send, s_send,
     xt, bct, ltr, d_recv, s_recv, inc_send, inc_recv, y_send, y_recv,
     xd_s, sp_out, e_run, run_s, runt_s, spread_s, spread_t, order_t, lcol, state, d_exp,
-    load_sem, x_ssem, x_rsem, b_ssem, b_rsem, l_ssem, l_rsem, d_ssem, d_rsem,
+    load_sem, x_ssem, x_rsem, b_ssem, b_rsem, f_ssem, l_ssem, l_rsem, d_ssem, d_rsem,
     s_ssem, s_rsem, i_ssem, i_rsem, y_ssem, y_rsem,
 ):
     t = lax.axis_index("tm")
     h = lax.axis_index("height")
-    z = t // 2
-    core = t % 2
 
     def remote(src, dst, ssem, rsem, **where):
         return pltpu.make_async_remote_copy(
@@ -78,25 +81,24 @@
             device_id=where, device_id_type=pl.DeviceIdType.MESH,
         )
 
-    def group_at(step):
-        return (z + 1 + step) % GROUPS
-
-    def lanes_of(group):
-        return pl.ds(pl.multiple_of(group * GL, 128), GL)
+    own_row, own_group = t // GROUPS, t % GROUPS
+
+    def lanes_of(index):
+        return pl.ds(pl.multiple_of(index * GL, 128), GL)
+
+    def half_lanes(start, half):
+        return pl.ds(pl.multiple_of(start + half * HALF, 128), HALF)
 
     loads = [
         pltpu.make_async_copy(tokens, tok_v, load_sem.at[0]),
         pltpu.make_async_copy(w_bc, w_bc_v, load_sem.at[1]),
         pltpu.make_async_copy(w_dt, w_dt_v, load_sem.at[2]),
     ]
-    for step in range(GROUPS):
-        where = lanes_of(group_at(step))
+    for step in range(4):
+        where = pl.ds(HALF * step, HALF)
         loads.append(pltpu.make_async_copy(w_in.at[:, where], w_in_v.at[:, where], load_sem.at[3 + step]))
-    for step in range(2):
-        where = pl.ds(INNER + 768 * step, 768)
-        loads.append(pltpu.make_async_copy(w_in.at[:, where], w_in_v.at[:, where], load_sem.at[7 + step]))
-    loads.append(pltpu.make_async_copy(w_out, w_out_v, load_sem.at[9]))
-    for load in loads:
+    loads.append(pltpu.make_async_copy(w_out, w_out_v, load_sem.at[7]))
+    for load in loads[:5]:
         load.start()
 
     barrier = pltpu.get_barrier_semaphore()
@@ -124,7 +126,7 @@
         rows = pl.ds(pl.multiple_of(k * 32, 32), 32)
         v = tok_v[rows, :].astype(F32)
         mean_square = jnp.mean(v * v, axis=-1, keepdims=True)
-        normed[rows, :] = (v * lax.rsqrt(mean_square + EPSILON) * gain[...]).astype(BF16)
+        normed[rows, :] = (v * lax.rsqrt(mean_square + EPSILON) * gain[...].reshape(1, D)).astype(BF16)
 
     loads[1].wait()
     bc = mm(normed[...], w_bc_v[...]).astype(BF16)
@@ -134,7 +136,7 @@
             at = 128 * f + 64 * r
             bct_send[r, f] = bc[at : at + 64, 2 * STATE :]
     loads[2].wait()
-    logits = mm(normed[...], w_dt_v[...]).astype(BF16).astype(F32)
+    logits = mm_rows(normed[...], w_dt_v[...]).astype(BF16).astype(F32)
     dt = softplus(logits + dt_bias[...])
     rates = jnp.concatenate([rate[0:1, :], rate[1:2, :]], axis=1)
     decay = -dt * rates * LOG2E
@@ -164,22 +166,36 @@
     dt_parts = parts(dt_s, 2)
     from_start = parts(jnp.exp2(run), 2)
 
+    for half in range(2):
+        loads[3 + half].wait()
+        if half == 1:
+            for load in loads[5:]:
+                load.start()
+        lanes = pl.ds(HALF * half, HALF)
+        xh = mm(normed[...], w_in_v[:, lanes]).astype(BF16)
+        x_all[0, :, lanes] = xh[:128]
+        x_all[1, :, lanes] = xh[128:]
+
     pl.semaphore_wait(barrier, TM - 1 + HT - 1)
 
+    def l_copy(to):
+        return remote(l_send.at[to % GROUPS, to // GROUPS], ltr.at[t], l_ssem.at[to], l_rsem.at[t], tm=to)
+
     def bc_copy(to):
-        return remote(bct_send.at[to % 2], bct.at[t], b_ssem.at[to], b_rsem.at[t], tm=to)
-
-    def l_copy(to):
-        return remote(l_send.at[to // 2, to % 2], ltr.at[t], l_ssem.at[to], l_rsem.at[t], tm=to)
-
-    @pl.loop(1, TM)
-    def _(k):
-        to = (t + k) % TM
-        l_copy(to).start()
-        bc_copy(to).start()
-
-    bct[t] = bct_send[core]
-    ltr[t] = l_send[z, core]
+        return remote(bct_send.at[to // GROUPS], bct.at[t], b_ssem.at[to], b_rsem.at[t], tm=to)
+
+    def bc_pass(source):
+        return remote(bct.at[source], bct.at[source], f_ssem.at[source], b_rsem.at[source], tm=t ^ 1)
+
+    def chunk_of(chunk):
+        return pl.ds(pl.multiple_of(chunk * CHUNK_COLS, CHUNK_COLS), CHUNK_COLS)
+
+    def x_copy(to, chunk):
+        rows = pl.ds(pl.multiple_of((to // GROUPS) * COLS + chunk * CHUNK_COLS, CHUNK_COLS), CHUNK_COLS)
+        return remote(
+            x_all.at[:, rows, lanes_of(to % GROUPS)], xt.at[t, :, chunk_of(chunk)],
+            x_ssem.at[to], x_rsem.at[chunk, t], tm=to,
+        )
 
     def owned(p):
         return p // 8, pl.ds(pl.multiple_of((p % 8) * 16, 16), 16)
@@ -187,73 +203,73 @@
     def d_copy(to):
         return remote(d_send.at[to // 8], d_recv.at[h], d_ssem.at[to], d_rsem.at[h], height=to)
 
+    bc_copy(t ^ 1).start()
+
+    @pl.loop(1, 4)
+    def _(k):
+        bc_copy((t + 2 * k) % TM).start()
+
+    @pl.loop(1, TM)
+    def _(k):
+        l_copy((t + k) % TM).start()
+
+    @pl.loop(0, CHUNKS)
+    def _(chunk):
+        @pl.loop(1, TM)
+        def _(k):
+            x_copy((t + k) % TM, chunk).start()
+
     @pl.loop(1, HT)
     def _(k):
         d_copy((h + k) % HT).start()
 
+    bct[t] = bct_send[own_row]
+    ltr[t] = l_send[own_group, own_row]
     d_recv[h] = d_send[h // 8]
-
-    def x_source(to):
-        rows = pl.ds(pl.multiple_of((to % 2) * COLS, COLS), COLS)
-        return x_all.at[:, rows, lanes_of(to // 2)]
-
-    def x_copy(to):
-        return remote(x_source(to), xt.at[t], x_ssem.at[to], x_rsem.at[t], tm=to)
-
-    for step in range(GROUPS):
-        group = group_at(step)
-        loads[3 + step].wait()
-        xg = mm(normed[...], w_in_v[:, lanes_of(group)]).astype(BF16)
-        x_all[0, :, lanes_of(group)] = xg[:128]
-        x_all[1, :, lanes_of(group)] = xg[128:]
-        for c in range(2):
-            to = group * 2 + c
-            if step < GROUPS - 1:
-                x_copy(to).start()
-            else:
-                @pl.when(to != t)
-                def _():
-                    x_copy(to).start()
-
-                @pl.when(to == t)
-                def _():
-                    for f in range(2):
-                        xt[t, f] = xg[128 * f + COLS * c : 128 * f + COLS * c + COLS]
-
-    for g in range(GROUPS):
-        lanes = pl.ds(GL * g, GL)
-        spread = spread_s[0:64, lanes]
-        weight = mm(to_end, spread)
-        steps = mm(dt_parts, spread)
-        e_run[:, lanes] = mm(from_start, spread)
-        for f in range(2):
-            rows = slice(128 * f, 128 * f + 128)
-            x = x_all[f, :, lanes].astype(F32)
-            xd_s[f, :, lanes] = (x * steps[rows]).astype(BF16)
-            s_send[f, :, lanes] = mm_tokens(
-                bc_s[rows, :STATE], (x * weight[rows]).astype(BF16)
-            ).astype(BF16)
-
-    def s_copy(to):
+    own_rows = pl.ds(pl.multiple_of(own_row * COLS, COLS), COLS)
+    for f in range(2):
+        xt[t, f] = x_all[f, own_rows, lanes_of(own_group)]
+
+    def s_copy(to, half):
         f, rows = owned(to)
-        return remote(s_send.at[f, rows], s_recv.at[h], s_ssem.at[to], s_rsem.at[h], height=to)
-
-    @pl.loop(1, HT)
-    def _(k):
-        s_copy((h + k) % HT).start()
-
-    own_f, own_rows = owned(h)
-    s_recv[h] = s_send[own_f, own_rows, :]
-
-    for step in range(2):
-        loads[7 + step].wait()
-
-        @pl.loop(0, 2)
-        def _(k):
-            lanes = pl.ds(pl.multiple_of(768 * step + 384 * k, 128), 384)
-            source = pl.ds(pl.multiple_of(INNER + 768 * step + 384 * k, 128), 384)
-            v = mm(normed[...], w_in_v[:, source]).astype(BF16).astype(F32)
-            gate[:, lanes] = v / (1.0 + jnp.exp(-v))
+        return remote(s_send.at[half, f, rows], s_recv.at[half, h], s_ssem.at[to], s_rsem.at[half, h], height=to)
+
+    own_f, own_n = owned(h)
+    for half in range(2):
+        for part in range(2):
+            lanes = pl.ds(HALF * half + GL * part, GL)
+            spread = spread_s[0:64, lanes]
+            weight = mm(to_end, spread)
+            steps = mm(dt_parts, spread)
+            e_run[:, lanes] = mm(from_start, spread)
+            for f in range(2):
+                rows = slice(128 * f, 128 * f + 128)
+                x = x_all[f, :, lanes].astype(F32)
+                xd_s[f, :, lanes] = (x * steps[rows]).astype(BF16)
+                s_send[half, f, :, pl.ds(GL * part, GL)] = mm_tokens(
+                    bc_s[rows, :STATE], (x * weight[rows]).astype(BF16)
+                ).astype(BF16)
+
+        @pl.loop(1, HT)
+        def _(k):
+            s_copy((h + k) % HT, half).start()
+
+        s_recv[half, h] = s_send[half, own_f, own_n, :]
+
+    @pl.loop(0, 4)
+    def _(k):
+        for step in range(2):
+            @pl.when(k == 2 * step)
+            def _():
+                loads[5 + step].wait()
+        v = mm(normed[...], w_in_v[:, pl.ds(pl.multiple_of(INNER + GL * k, 128), GL)]).astype(BF16).astype(F32)
+        gate[:, lanes_of(k)] = v / (1.0 + jnp.exp(-v))
+
+    @pl.loop(1, 4)
+    def _(k):
+        source = (t + 2 * k) % TM
+        remote(bct_send.at[0], bct.at[source], b_ssem.at[source], b_rsem.at[source], tm=source).wait_recv()
+        bc_pass(source).start()
 
     half = iota((128, 128), 1) < 64
     causal = iota((128, 128), 0) >= iota((128, 128), 1)
@@ -262,7 +278,7 @@
     def _(f):
         rows = pl.ds(pl.multiple_of(f * 128, 128), 128)
         b, c = bc_s[rows, :STATE], bc_s[rows, STATE:]
-        scores = lax.dot_general(c, b, (((1,), (1,)), ((), ())), preferred_element_type=F32)
+        scores = mm_rows(c, b)
         scores = jnp.where(causal, scores, 0.0)
         run_f, runt_f = run_s[rows, :], runt_s[f]
         for pair in range(HEADS // 2):
@@ -282,43 +298,50 @@
         remote(d_send.at[0], d_recv.at[source], d_ssem.at[source], d_rsem.at[source], height=source).wait_recv()
 
     totals = jnp.concatenate([d_recv[k, 0:1, :32] for k in range(HT)], axis=0)
-    d_exp[...] = mm(parts(totals, 3), spread_s[...])
-
-    @pl.loop(1, HT)
-    def _(k):
-        source = (h + k) % HT
-        remote(s_send.at[0, pl.ds(0, 16)], s_recv.at[source], s_ssem.at[source], s_rsem.at[source], height=source).wait_recv()
-
-    before = jnp.zeros((16, INNER), F32)
-    for k in range(HT):
-        inc_send[k] = before.astype(BF16)
-        if k < HT - 1:
-            before = before * d_exp[k : k + 1, :] + s_recv[k].astype(F32)
-
-    def i_copy(to):
+    totals = parts(totals, 3)
+    for half in range(2):
+        d_exp[half] = mm(totals, spread_s[:, pl.ds(HALF * half, HALF)])
+
+    def i_copy(to, half):
         f, rows = owned(h)
-        return remote(inc_send.at[to], inc_recv.at[f, rows], i_ssem.at[to], i_rsem.at[h], height=to)
-
-    @pl.loop(1, HT)
-    def _(k):
-        i_copy((h + k) % HT).start()
-
-    inc_recv[own_f, own_rows, :] = inc_send[h]
+        return remote(
+            inc_send.at[half, to], inc_recv.at[half, f, rows], i_ssem.at[to], i_rsem.at[half, h], height=to
+        )
+
+    def prefix(half):
+        @pl.loop(1, HT)
+        def _(k):
+            source = (h + k) % HT
+            remote(
+                s_send.at[0, 0, pl.ds(0, 16)], s_recv.at[half, source],
+                s_ssem.at[source], s_rsem.at[half, source], height=source,
+            ).wait_recv()
+
+        before = jnp.zeros((16, HALF), F32)
+        for k in range(HT):
+            inc_send[half, k] = before.astype(BF16)
+            if k < HT - 1:
+                before = before * d_exp[half, k : k + 1, :] + s_recv[half, k].astype(F32)
+
+        @pl.loop(1, HT)
+        def _(k):
+            i_copy((h + k) % HT, half).start()
+
+        inc_recv[half, own_f, own_n, :] = inc_send[half, h]
 
     @pl.loop(1, TM)
     def _(k):
         source = (t + k) % TM
         remote(l_send.at[0, 0], ltr.at[source], l_ssem.at[source], l_rsem.at[source], tm=source).wait_recv()
+
+    @pl.loop(0, 4)
+    def _(k):
+        source = (t + 2 * k) % TM ^ 1
         remote(bct_send.at[0], bct.at[source], b_ssem.at[source], b_rsem.at[source], tm=source).wait_recv()
 
     columns = ltr[...].reshape(TM * 16, 128).T
     for s in range(TM):
         lcol[s] = columns[:, 16 * s : 16 * s + 16]
-
-    @pl.loop(1, TM)
-    def _(k):
-        source = (t + k) % TM
-        remote(x_all.at[:, pl.ds(0, COLS), pl.ds(0, GL)], xt.at[source], x_ssem.at[source], x_rsem.at[source], tm=source).wait_recv()
 
     state[...] = jnp.zeros_like(state)
 
@@ -329,7 +352,15 @@
 
     @pl.loop(0, CHUNKS)
     def _(chunk):
-        cols = pl.ds(pl.multiple_of(chunk * CHUNK_COLS, CHUNK_COLS), CHUNK_COLS)
+        cols = chunk_of(chunk)
+
+        @pl.loop(1, TM)
+        def _(k):
+            source = (t + k) % TM
+            remote(
+                x_all.at[:, pl.ds(0, CHUNK_COLS), pl.ds(0, GL)], xt.at[source, :, cols],
+                x_ssem.at[source], x_rsem.at[chunk, source], tm=source,
+            ).wait_recv()
 
         def tokens_of(f):
             return pl.ds(pl.multiple_of(f * COLS + chunk * CHUNK_COLS, CHUNK_COLS), CHUNK_COLS)
@@ -348,7 +379,7 @@
         weight = mm(parts(jnp.exp2(last - runs) * dtv, 2), spread_t[...])
         steps = mm(parts(dtv, 2), spread_t[...])
         grown = mm(parts(jnp.exp2(runs), 2), spread_t[...])
-        scores = lax.dot_general(c, b, (((1,), (1,)), ((), ())), preferred_element_type=F32)
+        scores = mm_rows(c, b)
         scores = scores * order_t[...].astype(F32)
         xf = x.astype(F32)
         xd = (xf * steps).astype(BF16)
@@ -374,19 +405,28 @@
         def _(k):
             y_copy((t + k) % TM, cols).start()
 
+        @pl.when(chunk < 2)
+        def _():
+            prefix(chunk)
+
     y_recv[t] = y_send[t]
 
-    @pl.loop(1, HT)
-    def _(k):
-        source = (h + k) % HT
-        f, rows = owned(source)
-        remote(inc_send.at[source], inc_recv.at[f, rows], i_ssem.at[source], i_rsem.at[source], height=source).wait_recv()
-
-    for f in range(2):
-        rows = slice(128 * f, 128 * f + 128)
-        for g in range(GROUPS):
-            lanes = slice(GL * g, GL * g + GL)
-            sp_out[rows, lanes] += e_run[rows, lanes] * mm(bc_s[rows, STATE:], inc_recv[f, :, lanes])
+    for half in range(2):
+        @pl.loop(1, HT)
+        def _(k):
+            source = (h + k) % HT
+            f, rows = owned(source)
+            remote(
+                inc_send.at[half, source], inc_recv.at[half, f, rows],
+                i_ssem.at[source], i_rsem.at[half, source], height=source,
+            ).wait_recv()
+
+        for f in range(2):
+            rows = slice(128 * f, 128 * f + 128)
+            for part in range(2):
+                lanes = pl.ds(HALF * half + GL * part, GL)
+                earlier = mm(bc_s[rows, STATE:], inc_recv[half, f, :, pl.ds(GL * part, GL)])
+                sp_out[rows, lanes] += e_run[rows, lanes] * earlier
 
     @pl.loop(1, TM)
     def _(k):
@@ -398,32 +438,39 @@
         f, r, part = k // 4, (k // 2) % 2, k % 2
         rows = pl.ds(pl.multiple_of(k * 32, 32), 32)
         cols = pl.ds(pl.multiple_of(part * 32, 32), 32)
-        temporal = jnp.concatenate([y_recv[2 * g + r, f, cols, :] for g in range(GROUPS)], axis=1)
+        temporal = jnp.concatenate([y_recv[GROUPS * r + g, f, cols, :] for g in range(GROUPS)], axis=1)
         gated = (sp_out[rows, :] + temporal.astype(F32)) * gate[rows, :]
         mean_square = jnp.mean(gated * gated, axis=-1, keepdims=True)
-        normed[rows, :] = (gated * lax.rsqrt(mean_square + EPSILON) * out_gain[...]).astype(BF16)
-
-    loads[9].wait()
+        normed[rows, :] = (gated * lax.rsqrt(mean_square + EPSILON) * out_gain[...].reshape(1, INNER)).astype(BF16)
+
+    loads[7].wait()
 
     @pl.loop(0, 4)
     def _(k):
         lanes = pl.ds(pl.multiple_of(384 * k, 128), 384)
         out[:, lanes] = mm(normed[...], w_out_v[:, lanes]).astype(BF16)
 
+    bc_copy(t ^ 1).wait_send()
+
+    @pl.loop(1, 4)
+    def _(k):
+        bc_copy((t + 2 * k) % TM).wait_send()
+        bc_pass((t + 2 * k) % TM).wait_send()
+
     @pl.loop(1, TM)
     def _(k):
         to = (t + k) % TM
         l_copy(to).wait_send()
-        bc_copy(to).wait_send()
-        x_copy(to).wait_send()
+        remote(xt.at[to], xt.at[to], x_ssem.at[to], x_rsem.at[0, to], tm=to).wait_send()
         y_copy(to, pl.ds(0, COLS)).wait_send()
 
     @pl.loop(1, HT)
     def _(k):
         to = (h + k) % HT
         d_copy(to).wait_send()
-        s_copy(to).wait_send()
-        i_copy(to).wait_send()
+        for half in range(2):
+            s_copy(to, half).wait_send()
+            i_copy(to, half).wait_send()
 
 
 def per_device(tokens, norm_gain, in_weight, bc_weight, dt_weight, dt_bias, decay_rate, out_gain, out_weight):
@@ -439,7 +486,7 @@
             pltpu.VMEM((TOK, D), BF16),
             pltpu.VMEM((D, 2 * INNER), BF16),
             pltpu.VMEM((D, 4 * STATE), BF16),
-            pltpu.VMEM((D, 2 * HEADS), BF16),
+            pltpu.VMEM((2 * HEADS, D), BF16),
             pltpu.VMEM((INNER, D), BF16),
             pltpu.VMEM((TOK, D), BF16),
             pltpu.VMEM((2, 128, INNER), BF16),
@@ -448,14 +495,14 @@
             pltpu.VMEM((2, 2, COLS, 2 * STATE), BF16),
             pltpu.VMEM((GROUPS, 2, 16, 128), F32),
             pltpu.VMEM((2, 8, 128), F32),
-            pltpu.VMEM((2, STATE, INNER), BF16),
+            pltpu.VMEM((2, 2, STATE, HALF), BF16),
             pltpu.VMEM((TM, 2, COLS, GL), BF16),
             pltpu.VMEM((TM, 2, COLS, 2 * STATE), BF16),
             pltpu.VMEM((TM, 16, 128), F32),
             pltpu.VMEM((HT, 8, 128), F32),
-            pltpu.VMEM((HT, 16, INNER), BF16),
-            pltpu.VMEM((HT, 16, INNER), BF16),
-            pltpu.VMEM((2, STATE, INNER), BF16),
+            pltpu.VMEM((2, HT, 16, HALF), BF16),
+            pltpu.VMEM((2, HT, 16, HALF), BF16),
+            pltpu.VMEM((2, 2, STATE, HALF), BF16),
             pltpu.VMEM((TM, 2, COLS, GL), BF16),
             pltpu.VMEM((TM, 2, COLS, GL), BF16),
             pltpu.VMEM((2, 128, INNER), BF16),
@@ -468,10 +515,14 @@
             pltpu.VMEM((TOK, TOK), BF16),
             pltpu.VMEM((TM, 128, 16), F32),
             pltpu.VMEM((STATE, GL), F32),
-            pltpu.VMEM((HT, INNER), F32),
-            dma((10,)),
-            dma((TM,)), dma((TM,)), dma((TM,)), dma((TM,)), dma((TM,)), dma((TM,)),
-            dma((HT,)), dma((HT,)), dma((HT,)), dma((HT,)), dma((HT,)), dma((HT,)),
+            pltpu.VMEM((2, HT, HALF), F32),
+            dma((8,)),
+            dma((TM,)), dma((CHUNKS, TM)),
+            dma((TM,)), dma((TM,)), dma((TM,)),
+            dma((TM,)), dma((TM,)),
+            dma((HT,)), dma((HT,)),
+            dma((HT,)), dma((2, HT)),
+            dma((HT,)), dma((2, HT)),
             dma((TM,)), dma((TM,)),
         ],
         compiler_params=pltpu.CompilerParams(
@@ -480,13 +531,13 @@
         name="layer",
     )(
         tokens.reshape(TOK, D),
-        norm_gain.reshape(1, D),
+        norm_gain,
         in_weight,
         bc_weight,
-        dt_weight,
+        dt_weight.T,
         dt_bias.reshape(1, 2 * HEADS),
         decay_rate,
-        out_gain.reshape(1, INNER),
+        out_gain,
         out_weight,
     )
     return out.reshape(tokens.shape)

time: 51.2 us -> 43.5 us (0.85)
  local copies, waits for them, and re-layouts: 6.48 us -> 2.06 us
  Pallas kernels: 44.4 us -> 41.3 us
    pallas_call x1, Pallas kernels: 44.4 us -> 41.3 us  [per_device(): pl.pallas_call(kernel, out_shape=jax.ShapeDtypeStruct((TOK, D), BF16), in...]
    reshape x2 -> x0, local copies, waits for them, and re-layouts: 2.58 us -> none  [the longest x1 1.3 us: per_device(): out_gain.reshape(1, INNER)]
    unnamed x2 -> x1, local copies, waits for them, and re-layouts: 3.89 us -> 2.06 us
where the time goes in v2:
time: 43.5 us; the launch traced here: 43.3 us
  Pallas kernels  41.3 us (95%)
  local copies, waits for them, and re-layouts  2.06 us (5%)
    pallas_call x1, Pallas kernels, per_device(): pl.pallas_call(kernel, out_shape=jax.ShapeDtypeStruct((TOK, D), BF16), in...  41.3 us
    unnamed x1, local copies, waits for them, and re-layouts  2.06 us

profile of v2, /device:TPU:1, one launch (start us, length us, event | category | flops | bytes accessed | tf_op | source)
XLA Modules:
  0.0 43.3 jit_solution(12538598648963120127)
XLA Ops:
  0.0 41.3 %layer.1 = bf16[256,1536]{1,0:T(8,128)(2,1)} custom-call(bf16[256,1536]{1,0:T(8,128)(2,1)} %bitcast.5, f32[1536]{0:T(1024)} %gain.1, bf16[1536,3072]{1,0:T(8,128)(2,1)} %w_in.1, bf16[1536,512]{1,0:T(8,128)(2,1)} %w_bc.1, bf16[48,1536]{1,0:T(8,128)(2,1)} %bitcast.6, f32[1,48]{1,0:T(1,128)} %bitcast.7, f32[2,24]{1,0:T(2,128)} %rate.1, f32[1536]{0:T(1024)} %out_gain.1, ...), custom_call_target="tpu_custom_call" | custom-call | tf_op jit(solution)/shard_map/layer/pallas_call | solution.py:480
  41.3 2.1 %copy.11 = bf16[2,2,64,1536]{3,2,1,0:T(8,128)(2,1)} copy(bf16[2,2,64,1536]{3,2,1,0:T(8,128)(2,1)} %bitcast.4) | data formatting | bytes 1572864

commit v3 on v2

--- a/solution.py
+++ b/solution.py
@@ -64,8 +64,8 @@
 
 
 def kernel(
-    tokens, gain, w_in, w_bc, w_dt, dt_bias, rate, out_gain, w_out, out,
-    tok_v, w_in_v, w_bc_v, w_dt_v, w_out_v,
+    tokens, gain, w_in, w_bc, w_dt, dt_bias, rate, out_gain, out,
+    tok_v, w_in_v, w_bc_v, w_dt_v,
     normed, x_all, gate, bc_s, bct_send, l_send, d_send, s_send,
     xt, bct, ltr, d_recv, s_recv, inc_send, inc_recv, y_send, y_recv,
     xd_s, sp_out, e_run, run_s, runt_s, spread_s, spread_t, order_t, lcol, state, d_exp,
@@ -97,7 +97,6 @@
     for step in range(4):
         where = pl.ds(HALF * step, HALF)
         loads.append(pltpu.make_async_copy(w_in.at[:, where], w_in_v.at[:, where], load_sem.at[3 + step]))
-    loads.append(pltpu.make_async_copy(w_out, w_out_v, load_sem.at[7]))
     for load in loads[:5]:
         load.start()
 
@@ -135,7 +134,56 @@
         for r in range(2):
             at = 128 * f + 64 * r
             bct_send[r, f] = bc[at : at + 64, 2 * STATE :]
+
+    pl.semaphore_wait(barrier, TM - 1 + HT - 1)
+
+    def bc_copy(to):
+        return remote(bct_send.at[to // GROUPS], bct.at[t], b_ssem.at[to], b_rsem.at[t], tm=to)
+
+    def bc_pass(source):
+        return remote(bct.at[source], bct.at[source], f_ssem.at[source], b_rsem.at[source], tm=t ^ 1)
+
+    @pl.loop(1, 4)
+    def _(k):
+        bc_copy((t + 2 * k) % TM).start()
+
+    bc_copy(t ^ 1).start()
+    bct[t] = bct_send[own_row]
+
+    def l_copy(to):
+        return remote(l_send.at[to % GROUPS, to // GROUPS], ltr.at[t], l_ssem.at[to], l_rsem.at[t], tm=to)
+
+    def chunk_of(chunk):
+        return pl.ds(pl.multiple_of(chunk * CHUNK_COLS, CHUNK_COLS), CHUNK_COLS)
+
+    def x_copy(to, chunk):
+        rows = pl.ds(pl.multiple_of((to // GROUPS) * COLS + chunk * CHUNK_COLS, CHUNK_COLS), CHUNK_COLS)
+        return remote(
+            x_all.at[:, rows, lanes_of(to % GROUPS)], xt.at[t, :, chunk_of(chunk)],
+            x_ssem.at[to], x_rsem.at[chunk, t], tm=to,
+        )
+
+    def owned(p):
+        return p // 8, pl.ds(pl.multiple_of((p % 8) * 16, 16), 16)
+
+    own_f, own_n = owned(h)
+
+    def d_copy(to):
+        return remote(d_send.at[to // 8], d_recv.at[h], d_ssem.at[to], d_rsem.at[h], height=to)
+
+    def s_copy(to, half):
+        f, rows = owned(to)
+        return remote(s_send.at[half, f, rows], s_recv.at[half, h], s_ssem.at[to], s_rsem.at[half, h], height=to)
+
+    def x_half(half):
+        lanes = pl.ds(HALF * half, HALF)
+        xh = mm(normed[...], w_in_v[:, lanes]).astype(BF16)
+        x_all[0, :, lanes] = xh[:128]
+        x_all[1, :, lanes] = xh[128:]
+
     loads[2].wait()
+    loads[3].wait()
+    x_half(0)
     logits = mm_rows(normed[...], w_dt_v[...]).astype(BF16).astype(F32)
     dt = softplus(logits + dt_bias[...])
     rates = jnp.concatenate([rate[0:1, :], rate[1:2, :]], axis=1)
@@ -166,48 +214,33 @@
     dt_parts = parts(dt_s, 2)
     from_start = parts(jnp.exp2(run), 2)
 
-    for half in range(2):
-        loads[3 + half].wait()
-        if half == 1:
-            for load in loads[5:]:
-                load.start()
-        lanes = pl.ds(HALF * half, HALF)
-        xh = mm(normed[...], w_in_v[:, lanes]).astype(BF16)
-        x_all[0, :, lanes] = xh[:128]
-        x_all[1, :, lanes] = xh[128:]
-
-    pl.semaphore_wait(barrier, TM - 1 + HT - 1)
-
-    def l_copy(to):
-        return remote(l_send.at[to % GROUPS, to // GROUPS], ltr.at[t], l_ssem.at[to], l_rsem.at[t], tm=to)
-
-    def bc_copy(to):
-        return remote(bct_send.at[to // GROUPS], bct.at[t], b_ssem.at[to], b_rsem.at[t], tm=to)
-
-    def bc_pass(source):
-        return remote(bct.at[source], bct.at[source], f_ssem.at[source], b_rsem.at[source], tm=t ^ 1)
-
-    def chunk_of(chunk):
-        return pl.ds(pl.multiple_of(chunk * CHUNK_COLS, CHUNK_COLS), CHUNK_COLS)
-
-    def x_copy(to, chunk):
-        rows = pl.ds(pl.multiple_of((to // GROUPS) * COLS + chunk * CHUNK_COLS, CHUNK_COLS), CHUNK_COLS)
-        return remote(
-            x_all.at[:, rows, lanes_of(to % GROUPS)], xt.at[t, :, chunk_of(chunk)],
-            x_ssem.at[to], x_rsem.at[chunk, t], tm=to,
-        )
-
-    def owned(p):
-        return p // 8, pl.ds(pl.multiple_of((p % 8) * 16, 16), 16)
-
-    def d_copy(to):
-        return remote(d_send.at[to // 8], d_recv.at[h], d_ssem.at[to], d_rsem.at[h], height=to)
-
-    bc_copy(t ^ 1).start()
-
-    @pl.loop(1, 4)
-    def _(k):
-        bc_copy((t + 2 * k) % TM).start()
+    def state_half(half):
+        for part in range(2):
+            lanes = pl.ds(HALF * half + GL * part, GL)
+            spread = spread_s[0:64, lanes]
+            weight = mm(to_end, spread)
+            for f in range(2):
+                rows = slice(128 * f, 128 * f + 128)
+                x = x_all[f, :, lanes].astype(F32)
+                s_send[half, f, :, pl.ds(GL * part, GL)] = mm_tokens(
+                    bc_s[rows, :STATE], (x * weight[rows]).astype(BF16)
+                ).astype(BF16)
+
+        @pl.loop(1, HT)
+        def _(k):
+            s_copy((h + k) % HT, half).start()
+
+        s_recv[half, h] = s_send[half, own_f, own_n, :]
+
+    @pl.loop(1, HT)
+    def _(k):
+        d_copy((h + k) % HT).start()
+
+    state_half(0)
+    loads[4].wait()
+    for load in loads[5:]:
+        load.start()
+    x_half(1)
 
     @pl.loop(1, TM)
     def _(k):
@@ -219,42 +252,20 @@
         def _(k):
             x_copy((t + k) % TM, chunk).start()
 
-    @pl.loop(1, HT)
-    def _(k):
-        d_copy((h + k) % HT).start()
-
-    bct[t] = bct_send[own_row]
+    state_half(1)
+
     ltr[t] = l_send[own_group, own_row]
     d_recv[h] = d_send[h // 8]
     own_rows = pl.ds(pl.multiple_of(own_row * COLS, COLS), COLS)
     for f in range(2):
         xt[t, f] = x_all[f, own_rows, lanes_of(own_group)]
 
-    def s_copy(to, half):
-        f, rows = owned(to)
-        return remote(s_send.at[half, f, rows], s_recv.at[half, h], s_ssem.at[to], s_rsem.at[half, h], height=to)
-
-    own_f, own_n = owned(h)
-    for half in range(2):
-        for part in range(2):
-            lanes = pl.ds(HALF * half + GL * part, GL)
-            spread = spread_s[0:64, lanes]
-            weight = mm(to_end, spread)
-            steps = mm(dt_parts, spread)
-            e_run[:, lanes] = mm(from_start, spread)
-            for f in range(2):
-                rows = slice(128 * f, 128 * f + 128)
-                x = x_all[f, :, lanes].astype(F32)
-                xd_s[f, :, lanes] = (x * steps[rows]).astype(BF16)
-                s_send[half, f, :, pl.ds(GL * part, GL)] = mm_tokens(
-                    bc_s[rows, :STATE], (x * weight[rows]).astype(BF16)
-                ).astype(BF16)
-
-        @pl.loop(1, HT)
-        def _(k):
-            s_copy((h + k) % HT, half).start()
-
-        s_recv[half, h] = s_send[half, own_f, own_n, :]
+    for part in range(4):
+        lanes = pl.ds(GL * part, GL)
+        steps = mm(dt_parts, spread_s[0:64, lanes])
+        e_run[:, lanes] = mm(from_start, spread_s[0:64, lanes])
+        for f in range(2):
+            xd_s[f, :, lanes] = (x_all[f, :, lanes].astype(F32) * steps[128 * f : 128 * f + 128]).astype(BF16)
 
     @pl.loop(0, 4)
     def _(k):
@@ -292,15 +303,16 @@
             both_x = jnp.concatenate([jnp.where(half, x, none), jnp.where(half, none, x)], axis=0)
             sp_out[rows, lanes] = mm(jnp.concatenate(weights, axis=1), both_x)
 
-    @pl.loop(1, HT)
-    def _(k):
-        source = (h + k) % HT
-        remote(d_send.at[0], d_recv.at[source], d_ssem.at[source], d_rsem.at[source], height=source).wait_recv()
-
-    totals = jnp.concatenate([d_recv[k, 0:1, :32] for k in range(HT)], axis=0)
-    totals = parts(totals, 3)
-    for half in range(2):
-        d_exp[half] = mm(totals, spread_s[:, pl.ds(HALF * half, HALF)])
+    def band_decays():
+        @pl.loop(1, HT)
+        def _(k):
+            source = (h + k) % HT
+            remote(d_send.at[0], d_recv.at[source], d_ssem.at[source], d_rsem.at[source], height=source).wait_recv()
+
+        totals = jnp.concatenate([d_recv[k, 0:1, :32] for k in range(HT)], axis=0)
+        totals = parts(totals, 3)
+        for half in range(2):
+            d_exp[half] = mm(totals, spread_s[:, pl.ds(HALF * half, HALF)])
 
     def i_copy(to, half):
         f, rows = owned(h)
@@ -345,9 +357,9 @@
 
     state[...] = jnp.zeros_like(state)
 
-    def y_copy(to, cols):
+    def y_copy(to, cols, half):
         return remote(
-            y_send.at[to, :, cols], y_recv.at[t, :, cols], y_ssem.at[to], y_rsem.at[t], tm=to
+            y_send.at[to, :, cols], y_recv.at[t, :, cols], y_ssem.at[to], y_rsem.at[half, t], tm=to
         )
 
     @pl.loop(0, CHUNKS)
@@ -403,7 +415,11 @@
 
         @pl.loop(1, TM)
         def _(k):
-            y_copy((t + k) % TM, cols).start()
+            y_copy((t + k) % TM, cols, chunk // 2).start()
+
+        @pl.when(chunk == 0)
+        def _():
+            band_decays()
 
         @pl.when(chunk < 2)
         def _():
@@ -428,27 +444,26 @@
                 earlier = mm(bc_s[rows, STATE:], inc_recv[half, f, :, pl.ds(GL * part, GL)])
                 sp_out[rows, lanes] += e_run[rows, lanes] * earlier
 
-    @pl.loop(1, TM)
-    def _(k):
-        source = (t + k) % TM
-        remote(y_send.at[source], y_recv.at[source], y_ssem.at[source], y_rsem.at[source], tm=source).wait_recv()
-
-    @pl.loop(0, 8)
-    def _(k):
-        f, r, part = k // 4, (k // 2) % 2, k % 2
-        rows = pl.ds(pl.multiple_of(k * 32, 32), 32)
+    @pl.loop(0, 2)
+    def _(part):
         cols = pl.ds(pl.multiple_of(part * 32, 32), 32)
-        temporal = jnp.concatenate([y_recv[GROUPS * r + g, f, cols, :] for g in range(GROUPS)], axis=1)
-        gated = (sp_out[rows, :] + temporal.astype(F32)) * gate[rows, :]
-        mean_square = jnp.mean(gated * gated, axis=-1, keepdims=True)
-        normed[rows, :] = (gated * lax.rsqrt(mean_square + EPSILON) * out_gain[...].reshape(1, INNER)).astype(BF16)
-
-    loads[7].wait()
-
-    @pl.loop(0, 4)
-    def _(k):
-        lanes = pl.ds(pl.multiple_of(384 * k, 128), 384)
-        out[:, lanes] = mm(normed[...], w_out_v[:, lanes]).astype(BF16)
+
+        @pl.loop(1, TM)
+        def _(k):
+            source = (t + k) % TM
+            remote(
+                y_send.at[source, :, cols], y_recv.at[source, :, cols],
+                y_ssem.at[source], y_rsem.at[part, source], tm=source,
+            ).wait_recv()
+
+        @pl.loop(0, 4)
+        def _(k):
+            f, r = k // 2, k % 2
+            rows = pl.ds(pl.multiple_of(k * COLS + part * 32, 32), 32)
+            temporal = jnp.concatenate([y_recv[GROUPS * r + g, f, cols, :] for g in range(GROUPS)], axis=1)
+            gated = (sp_out[rows, :] + temporal.astype(F32)) * gate[rows, :]
+            mean_square = jnp.mean(gated * gated, axis=-1, keepdims=True)
+            out[rows, :] = (gated * lax.rsqrt(mean_square + EPSILON) * out_gain[...].reshape(1, INNER)).astype(BF16)
 
     bc_copy(t ^ 1).wait_send()
 
@@ -462,7 +477,7 @@
         to = (t + k) % TM
         l_copy(to).wait_send()
         remote(xt.at[to], xt.at[to], x_ssem.at[to], x_rsem.at[0, to], tm=to).wait_send()
-        y_copy(to, pl.ds(0, COLS)).wait_send()
+        y_copy(to, pl.ds(0, COLS), 0).wait_send()
 
     @pl.loop(1, HT)
     def _(k):
@@ -477,17 +492,16 @@
     vmem = pl.BlockSpec(memory_space=pltpu.VMEM)
     hbm = pl.BlockSpec(memory_space=pl.ANY)
     dma = pltpu.SemaphoreType.DMA
-    out = pl.pallas_call(
+    normed_out = pl.pallas_call(
         kernel,
-        out_shape=jax.ShapeDtypeStruct((TOK, D), BF16),
-        in_specs=[hbm, vmem, hbm, hbm, hbm, vmem, vmem, vmem, hbm],
+        out_shape=jax.ShapeDtypeStruct((TOK, INNER), BF16),
+        in_specs=[hbm, vmem, hbm, hbm, hbm, vmem, vmem, vmem],
         out_specs=vmem,
         scratch_shapes=[
             pltpu.VMEM((TOK, D), BF16),
             pltpu.VMEM((D, 2 * INNER), BF16),
             pltpu.VMEM((D, 4 * STATE), BF16),
             pltpu.VMEM((2 * HEADS, D), BF16),
-            pltpu.VMEM((INNER, D), BF16),
             pltpu.VMEM((TOK, D), BF16),
             pltpu.VMEM((2, 128, INNER), BF16),
             pltpu.VMEM((TOK, INNER), F32),
@@ -523,7 +537,7 @@
             dma((HT,)), dma((HT,)),
             dma((HT,)), dma((2, HT)),
             dma((HT,)), dma((2, HT)),
-            dma((TM,)), dma((TM,)),
+            dma((TM,)), dma((2, TM)),
         ],
         compiler_params=pltpu.CompilerParams(
             collective_id=0, has_side_effects=True, vmem_limit_bytes=56 * 1024 * 1024
@@ -538,9 +552,8 @@
         dt_bias.reshape(1, 2 * HEADS),
         decay_rate,
         out_gain,
-        out_weight,
     )
-    return out.reshape(tokens.shape)
+    return mm(normed_out, out_weight).astype(BF16).reshape(tokens.shape)
 
 
 def solution(mesh):

time: 43.5 us -> 41.4 us (0.952)
  matrix products: 0 us -> 3.4 us
  Pallas kernels: 41.3 us -> 37.9 us
  local copies, waits for them, and re-layouts: 2.06 us -> 0.01 us
    pallas_call x1, Pallas kernels: 41.3 us -> 37.9 us  [per_device(): pl.pallas_call(kernel, out_shape=jax.ShapeDtypeStruct((TOK, INNER), BF16)...]
    dot_general x0 -> x1, matrix products: none -> 3.4 us  [mm(): return jnp.dot(a, b, preferred_element_type=F32)]
    unnamed x1 -> x2, local copies, waits for them, and re-layouts: 2.06 us -> 0.01 us
where the time goes in v3:
time: 41.4 us; the launch traced here: 41.3 us
  Pallas kernels  37.9 us (92%)
  matrix products  3.4 us (8%)
    pallas_call x1, Pallas kernels, per_device(): pl.pallas_call(kernel, out_shape=jax.ShapeDtypeStruct((TOK, INNER), BF16)...  37.9 us
    dot_general x1, matrix products, mm(): return jnp.dot(a, b, preferred_element_type=F32)  3.4 us

profile of v3, /device:TPU:1, one launch (start us, length us, event | category | flops | bytes accessed | tf_op | source)
XLA Modules:
  0.0 41.3 jit_solution(17094640111140786814)
XLA Ops:
  0.0 0.0 copy-start
  0.0 37.9 %layer.1 = bf16[256,1536]{1,0:T(8,128)(2,1)} custom-call(bf16[256,1536]{1,0:T(8,128)(2,1)} %bitcast.6, f32[1536]{0:T(1024)} %gain.1, bf16[1536,3072]{1,0:T(8,128)(2,1)} %w_in.1, bf16[1536,512]{1,0:T(8,128)(2,1)} %w_bc.1, bf16[48,1536]{1,0:T(8,128)(2,1)} %bitcast.7, f32[1,48]{1,0:T(1,128)} %bitcast.8, f32[2,24]{1,0:T(2,128)} %rate.1, f32[1536]{0:T(1024)} %out_gain.1), custom_call_target="tpu_custom_call" | custom-call | tf_op jit(solution)/shard_map/layer/pallas_call | solution.py:495
  37.9 0.0 copy-done
  37.9 3.4 %convolution_convert_fusion = bf16[256,1536]{1,0:T(8,128)(2,1)} fusion(bf16[256,1536]{1,0:T(8,128)(2,1)} %layer.1, bf16[1536,1536]{1,0:T(8,128)(2,1)S(1)} %copy-done), kind=kOutput, calls=%fused_computation | convolution fusion | flops 1208352768 | bytes 6291456 | tf_op jit(solution)/shard_map/dot_general | solution.py:32
Async XLA Ops:
  0.0 37.9 %copy-start = (bf16[1536,1536]{1,0:T(8,128)(2,1)S(1)}, bf16[1536,1536]{1,0:T(8,128)(2,1)}, u32[]{:S(2)}) copy-start(bf16[1536,1536]{1,0:T(8,128)(2,1)} %param.17) | copy-start | bytes 14155780

commit v4 on v3

--- a/solution.py
+++ b/solution.py
@@ -64,12 +64,13 @@
 
 
 def kernel(
-    tokens, gain, w_in, w_bc, w_dt, dt_bias, rate, out_gain, out,
-    tok_v, w_in_v, w_bc_v, w_dt_v,
-    normed, x_all, gate, bc_s, bct_send, l_send, d_send, s_send,
-    xt, bct, ltr, d_recv, s_recv, inc_send, inc_recv, y_send, y_recv,
+    tokens, gain_in, w_in, w_bc, w_dt, dt_bias_in, rate_in, out_gain_in, w_out, out,
+    gain, dt_bias, rate, out_gain,
+    tok_v, w_in_v, w_bc_v, w_dt_v, w_out_v,
+    normed, x_all, gate, bc_s, bct_send, l_send, s_send,
+    xt, bct, ltr, s_recv, inc_send, inc_recv, y_send, y_recv,
     xd_s, sp_out, e_run, run_s, runt_s, spread_s, spread_t, order_t, lcol, state, d_exp,
-    load_sem, x_ssem, x_rsem, b_ssem, b_rsem, f_ssem, l_ssem, l_rsem, d_ssem, d_rsem,
+    mixed_v, load_sem, small_sem, out_sem, x_ssem, x_rsem, b_ssem, b_rsem, f_ssem, l_ssem, l_rsem,
     s_ssem, s_rsem, i_ssem, i_rsem, y_ssem, y_rsem,
 ):
     t = lax.axis_index("tm")
@@ -97,8 +98,18 @@
     for step in range(4):
         where = pl.ds(HALF * step, HALF)
         loads.append(pltpu.make_async_copy(w_in.at[:, where], w_in_v.at[:, where], load_sem.at[3 + step]))
+    loads.append(pltpu.make_async_copy(w_out, w_out_v, load_sem.at[7]))
+    small = [
+        pltpu.make_async_copy(source, target, small_sem.at[k])
+        for k, (source, target) in enumerate(
+            ((gain_in, gain), (dt_bias_in, dt_bias), (rate_in, rate), (out_gain_in, out_gain))
+        )
+    ]
+    small[0].start()
     for load in loads[:5]:
         load.start()
+    for load in small[1:]:
+        load.start()
 
     barrier = pltpu.get_barrier_semaphore()
 
@@ -118,6 +129,7 @@
 
     order_t[...] = (place(iota((TOK, TOK), 0)) >= place(iota((TOK, TOK), 1))).astype(F32).astype(BF16)
 
+    small[0].wait()
     loads[0].wait()
 
     @pl.loop(0, 8)
@@ -168,12 +180,13 @@
 
     own_f, own_n = owned(h)
 
-    def d_copy(to):
-        return remote(d_send.at[to // 8], d_recv.at[h], d_ssem.at[to], d_rsem.at[h], height=to)
-
     def s_copy(to, half):
         f, rows = owned(to)
-        return remote(s_send.at[half, f, rows], s_recv.at[half, h], s_ssem.at[to], s_rsem.at[half, h], height=to)
+        lanes = pl.ds(0, HALF + 128 * (1 - half))
+        return remote(
+            s_send.at[half, f, rows, lanes], s_recv.at[half, h, :, lanes],
+            s_ssem.at[to], s_rsem.at[half, h], height=to,
+        )
 
     def x_half(half):
         lanes = pl.ds(HALF * half, HALF)
@@ -181,6 +194,8 @@
         x_all[0, :, lanes] = xh[:128]
         x_all[1, :, lanes] = xh[128:]
 
+    for load in small[1:]:
+        load.wait()
     loads[2].wait()
     loads[3].wait()
     x_half(0)
@@ -206,9 +221,8 @@
         runt_s[f] = jnp.concatenate([run[128 * f : 128 * f + 128], jnp.zeros((128, 96), F32)], axis=1).T[:32]
     ends = [run[127:128], run[255:256]]
     for f in range(2):
-        d_send[f] = jnp.broadcast_to(
-            jnp.concatenate([jnp.exp2(ends[f]), jnp.zeros((1, 96), F32)], axis=1), (8, 128)
-        )
+        total = jnp.concatenate([parts(jnp.exp2(ends[f]), 3).astype(F32), jnp.zeros((1, 32), F32)], axis=1)
+        s_send[0, f, :, HALF:] = jnp.broadcast_to(total, (STATE, 128)).astype(BF16)
     end = jnp.concatenate([jnp.broadcast_to(e, (128, 32)) for e in ends], axis=0)
     to_end = parts(jnp.exp2(end - run) * dt_s, 2)
     dt_parts = parts(dt_s, 2)
@@ -230,32 +244,32 @@
         def _(k):
             s_copy((h + k) % HT, half).start()
 
-        s_recv[half, h] = s_send[half, own_f, own_n, :]
-
-    @pl.loop(1, HT)
-    def _(k):
-        d_copy((h + k) % HT).start()
-
-    state_half(0)
+        lanes = pl.ds(0, HALF + 128 * (1 - half))
+        s_recv[half, h, :, lanes] = s_send[half, own_f, own_n, lanes]
+
     loads[4].wait()
     for load in loads[5:]:
         load.start()
     x_half(1)
 
+    def x_send(chunk):
+        @pl.loop(1, TM)
+        def _(k):
+            x_copy((t + k) % TM, chunk).start()
+
+    x_send(0)
+    state_half(0)
+    x_send(1)
+
     @pl.loop(1, TM)
     def _(k):
         l_copy((t + k) % TM).start()
 
-    @pl.loop(0, CHUNKS)
-    def _(chunk):
-        @pl.loop(1, TM)
-        def _(k):
-            x_copy((t + k) % TM, chunk).start()
-
     state_half(1)
+    x_send(2)
+    x_send(3)
 
     ltr[t] = l_send[own_group, own_row]
-    d_recv[h] = d_send[h // 8]
     own_rows = pl.ds(pl.multiple_of(own_row * COLS, COLS), COLS)
     for f in range(2):
         xt[t, f] = x_all[f, own_rows, lanes_of(own_group)]
@@ -304,13 +318,11 @@
             sp_out[rows, lanes] = mm(jnp.concatenate(weights, axis=1), both_x)
 
     def band_decays():
-        @pl.loop(1, HT)
-        def _(k):
-            source = (h + k) % HT
-            remote(d_send.at[0], d_recv.at[source], d_ssem.at[source], d_rsem.at[source], height=source).wait_recv()
-
-        totals = jnp.concatenate([d_recv[k, 0:1, :32] for k in range(HT)], axis=0)
-        totals = parts(totals, 3)
+        row = iota((HT, 128), 0)
+        totals = jnp.zeros((HT, 128), F32)
+        for k in range(HT):
+            totals = jnp.where(row == k, s_recv[0, k, :, HALF:].astype(F32), totals)
+        totals = totals[:, :96].astype(BF16)
         for half in range(2):
             d_exp[half] = mm(totals, spread_s[:, pl.ds(HALF * half, HALF)])
 
@@ -324,16 +336,20 @@
         @pl.loop(1, HT)
         def _(k):
             source = (h + k) % HT
+            lanes = pl.ds(0, HALF + 128 * (1 - half))
             remote(
-                s_send.at[0, 0, pl.ds(0, 16)], s_recv.at[half, source],
+                s_send.at[half, 0, pl.ds(0, 16), lanes], s_recv.at[half, source, :, lanes],
                 s_ssem.at[source], s_rsem.at[half, source], height=source,
             ).wait_recv()
+
+        if half == 0:
+            band_decays()
 
         before = jnp.zeros((16, HALF), F32)
         for k in range(HT):
             inc_send[half, k] = before.astype(BF16)
             if k < HT - 1:
-                before = before * d_exp[half, k : k + 1, :] + s_recv[half, k].astype(F32)
+                before = before * d_exp[half, k : k + 1, :] + s_recv[half, k, :, :HALF].astype(F32)
 
         @pl.loop(1, HT)
         def _(k):
@@ -417,13 +433,10 @@
         def _(k):
             y_copy((t + k) % TM, cols, chunk // 2).start()
 
-        @pl.when(chunk == 0)
-        def _():
-            band_decays()
-
-        @pl.when(chunk < 2)
-        def _():
-            prefix(chunk)
+        for half in range(2):
+            @pl.when(chunk == half)
+            def _():
+                prefix(half)
 
     y_recv[t] = y_send[t]
 
@@ -444,6 +457,10 @@
                 earlier = mm(bc_s[rows, STATE:], inc_recv[half, f, :, pl.ds(GL * part, GL)])
                 sp_out[rows, lanes] += e_run[rows, lanes] * earlier
 
+    def out_copy(part, k):
+        rows = pl.ds(pl.multiple_of(k * COLS + part * 32, 32), 32)
+        return pltpu.make_async_copy(mixed_v.at[part, k], out.at[rows], out_sem.at[part, k])
+
     @pl.loop(0, 2)
     def _(part):
         cols = pl.ds(pl.multiple_of(part * 32, 32), 32)
@@ -456,14 +473,35 @@
                 y_ssem.at[source], y_rsem.at[part, source], tm=source,
             ).wait_recv()
 
-        @pl.loop(0, 4)
-        def _(k):
+        for k in range(4):
             f, r = k // 2, k % 2
             rows = pl.ds(pl.multiple_of(k * COLS + part * 32, 32), 32)
             temporal = jnp.concatenate([y_recv[GROUPS * r + g, f, cols, :] for g in range(GROUPS)], axis=1)
             gated = (sp_out[rows, :] + temporal.astype(F32)) * gate[rows, :]
             mean_square = jnp.mean(gated * gated, axis=-1, keepdims=True)
-            out[rows, :] = (gated * lax.rsqrt(mean_square + EPSILON) * out_gain[...].reshape(1, INNER)).astype(BF16)
+            normed[32 * k : 32 * k + 32, :] = (
+                gated * lax.rsqrt(mean_square + EPSILON) * out_gain[...].reshape(1, INNER)
+            ).astype(BF16)
+
+        @pl.when(part == 0)
+        def _():
+            loads[7].wait()
+
+        @pl.loop(0, 2)
+        def _(k):
+            lanes = pl.ds(pl.multiple_of(HALF * k, 128), HALF)
+            mixed = mm(normed[0:128, :], w_out_v[:, lanes]).astype(BF16)
+            for block in range(4):
+                mixed_v[part, block, :, lanes] = mixed[32 * block : 32 * block + 32]
+
+        @pl.loop(0, 4)
+        def _(k):
+            out_copy(part, k).start()
+
+    @pl.loop(0, 4)
+    def _(k):
+        out_copy(0, k).wait()
+        out_copy(1, k).wait()
 
     bc_copy(t ^ 1).wait_send()
 
@@ -482,39 +520,43 @@
     @pl.loop(1, HT)
     def _(k):
         to = (h + k) % HT
-        d_copy(to).wait_send()
         for half in range(2):
             s_copy(to, half).wait_send()
             i_copy(to, half).wait_send()
 
 
 def per_device(tokens, norm_gain, in_weight, bc_weight, dt_weight, dt_bias, decay_rate, out_gain, out_weight):
-    vmem = pl.BlockSpec(memory_space=pltpu.VMEM)
     hbm = pl.BlockSpec(memory_space=pl.ANY)
     dma = pltpu.SemaphoreType.DMA
-    normed_out = pl.pallas_call(
+    def keep(v):
+        return pltpu.with_memory_space_constraint(v, pltpu.HBM)
+
+    mixed = pl.pallas_call(
         kernel,
-        out_shape=jax.ShapeDtypeStruct((TOK, INNER), BF16),
-        in_specs=[hbm, vmem, hbm, hbm, hbm, vmem, vmem, vmem],
-        out_specs=vmem,
+        out_shape=jax.ShapeDtypeStruct((TOK, D), BF16),
+        in_specs=[hbm] * 9,
+        out_specs=pl.BlockSpec(memory_space=pltpu.VMEM),
         scratch_shapes=[
+            pltpu.VMEM((D,), F32),
+            pltpu.VMEM((1, 2 * HEADS), F32),
+            pltpu.VMEM((2, HEADS), F32),
+            pltpu.VMEM((INNER,), F32),
             pltpu.VMEM((TOK, D), BF16),
             pltpu.VMEM((D, 2 * INNER), BF16),
             pltpu.VMEM((D, 4 * STATE), BF16),
             pltpu.VMEM((2 * HEADS, D), BF16),
+            pltpu.VMEM((INNER, D), BF16),
             pltpu.VMEM((TOK, D), BF16),
             pltpu.VMEM((2, 128, INNER), BF16),
             pltpu.VMEM((TOK, INNER), F32),
             pltpu.VMEM((TOK, 2 * STATE), BF16),
             pltpu.VMEM((2, 2, COLS, 2 * STATE), BF16),
             pltpu.VMEM((GROUPS, 2, 16, 128), F32),
-            pltpu.VMEM((2, 8, 128), F32),
-            pltpu.VMEM((2, 2, STATE, HALF), BF16),
+            pltpu.VMEM((2, 2, STATE, HALF + 128), BF16),
             pltpu.VMEM((TM, 2, COLS, GL), BF16),
             pltpu.VMEM((TM, 2, COLS, 2 * STATE), BF16),
             pltpu.VMEM((TM, 16, 128), F32),
-            pltpu.VMEM((HT, 8, 128), F32),
-            pltpu.VMEM((2, HT, 16, HALF), BF16),
+            pltpu.VMEM((2, HT, 16, HALF + 128), BF16),
             pltpu.VMEM((2, HT, 16, HALF), BF16),
             pltpu.VMEM((2, 2, STATE, HALF), BF16),
             pltpu.VMEM((TM, 2, COLS, GL), BF16),
@@ -530,30 +572,31 @@
             pltpu.VMEM((TM, 128, 16), F32),
             pltpu.VMEM((STATE, GL), F32),
             pltpu.VMEM((2, HT, HALF), F32),
-            dma((8,)),
+            pltpu.VMEM((2, 4, 32, D), BF16),
+            dma((8,)), dma((4,)), dma((2, 4)),
             dma((TM,)), dma((CHUNKS, TM)),
             dma((TM,)), dma((TM,)), dma((TM,)),
             dma((TM,)), dma((TM,)),
-            dma((HT,)), dma((HT,)),
             dma((HT,)), dma((2, HT)),
             dma((HT,)), dma((2, HT)),
             dma((TM,)), dma((2, TM)),
         ],
         compiler_params=pltpu.CompilerParams(
-            collective_id=0, has_side_effects=True, vmem_limit_bytes=56 * 1024 * 1024
+            collective_id=0, has_side_effects=True, vmem_limit_bytes=40 * 1024 * 1024
         ),
         name="layer",
     )(
-        tokens.reshape(TOK, D),
-        norm_gain,
-        in_weight,
-        bc_weight,
-        dt_weight.T,
-        dt_bias.reshape(1, 2 * HEADS),
-        decay_rate,
-        out_gain,
+        keep(tokens.reshape(TOK, D)),
+        keep(norm_gain),
+        keep(in_weight),
+        keep(bc_weight),
+        keep(dt_weight.T),
+        keep(dt_bias.reshape(1, 2 * HEADS)),
+        keep(decay_rate),
+        keep(out_gain),
+        keep(out_weight),
     )
-    return mm(normed_out, out_weight).astype(BF16).reshape(tokens.shape)
+    return mixed.reshape(tokens.shape)
 
 
 def solution(mesh):

time: 41.4 us -> 39.7 us (0.959)
  matrix products: 3.4 us -> 0 us
  local copies, waits for them, and re-layouts: 0.01 us -> 0.88 us
  Pallas kernels: 37.9 us -> 38.7 us
    dot_general x1 -> x0, matrix products: 3.4 us -> none  [mm(): return jnp.dot(a, b, preferred_element_type=F32)]
    unnamed x2 -> x1, local copies, waits for them, and re-layouts: 0.01 us -> 0.88 us
    pallas_call x1, Pallas kernels: 37.9 us -> 38.7 us  [per_device(): pl.pallas_call(kernel, out_shape=jax.ShapeDtypeStruct((TOK, D), BF16), in...]
where the time goes in v4:
time: 39.7 us; the launch traced here: 39.6 us
  Pallas kernels  38.7 us (97%)
  local copies, waits for them, and re-layouts  0.88 us (2%)
    pallas_call x1, Pallas kernels, per_device(): pl.pallas_call(kernel, out_shape=jax.ShapeDtypeStruct((TOK, D), BF16), in...  38.7 us
    unnamed x1, local copies, waits for them, and re-layouts  0.88 us

profile of v4, /device:TPU:1, one launch (start us, length us, event | category | flops | bytes accessed | tf_op | source)
XLA Modules:
  0.0 39.6 jit_solution(17657128797381873779)
XLA Ops:
  0.0 38.7 %layer.1 = bf16[256,1536]{1,0:T(8,128)(2,1)S(1)} custom-call(bf16[256,1536]{1,0:T(8,128)(2,1)} %bitcast.5, f32[1536]{0:T(1024)} %gain_in.1, bf16[1536,3072]{1,0:T(8,128)(2,1)} %w_in.1, bf16[1536,512]{1,0:T(8,128)(2,1)} %w_bc.1, bf16[48,1536]{1,0:T(8,128)(2,1)} %bitcast.6, f32[1,48]{1,0:T(1,128)} %bitcast.7, f32[2,24]{1,0:T(2,128)} %rate_in.1, ...), custom_call_target="tpu_custom_call" | custom-call | tf_op jit(solution)/shard_map/layer/pallas_call | solution.py:534
  38.7 0.9 %copy.11 = bf16[2,2,64,1536]{3,2,1,0:T(8,128)(2,1)} copy(bf16[2,2,64,1536]{3,2,1,0:T(8,128)(2,1)S(1)} %bitcast.4) | data formatting | bytes 1572864

commit v5 on v4

--- a/solution.py
+++ b/solution.py
@@ -70,7 +70,7 @@
     normed, x_all, gate, bc_s, bct_send, l_send, s_send,
     xt, bct, ltr, s_recv, inc_send, inc_recv, y_send, y_recv,
     xd_s, sp_out, e_run, run_s, runt_s, spread_s, spread_t, order_t, lcol, state, d_exp,
-    mixed_v, load_sem, small_sem, out_sem, x_ssem, x_rsem, b_ssem, b_rsem, f_ssem, l_ssem, l_rsem,
+    scale_v, scale_in, load_sem, small_sem, x_ssem, x_rsem, b_ssem, b_rsem, l_ssem, l_rsem,
     s_ssem, s_rsem, i_ssem, i_rsem, y_ssem, y_rsem,
 ):
     t = lax.axis_index("tm")
@@ -81,6 +81,12 @@
             src_ref=src, dst_ref=dst, send_sem=ssem, recv_sem=rsem,
             device_id=where, device_id_type=pl.DeviceIdType.MESH,
         )
+
+    def received(ref, sem):
+        remote(ref, ref, sem, sem, tm=t ^ 1).wait_recv()
+
+    def sent(ref, sem):
+        remote(ref, ref, sem, sem, tm=t ^ 1).wait_send()
 
     own_row, own_group = t // GROUPS, t % GROUPS
 
@@ -132,15 +138,13 @@
     small[0].wait()
     loads[0].wait()
 
-    @pl.loop(0, 8)
-    def _(k):
-        rows = pl.ds(pl.multiple_of(k * 32, 32), 32)
-        v = tok_v[rows, :].astype(F32)
-        mean_square = jnp.mean(v * v, axis=-1, keepdims=True)
-        normed[rows, :] = (v * lax.rsqrt(mean_square + EPSILON) * gain[...].reshape(1, D)).astype(BF16)
+    tok = tok_v[...].astype(F32)
+    normed[...] = (tok * gain[...].reshape(1, D)).astype(BF16)
+    scale = lax.rsqrt(jnp.mean(tok * tok, axis=-1, keepdims=True) + EPSILON)
+    scale_in[...] = scale
 
     loads[1].wait()
-    bc = mm(normed[...], w_bc_v[...]).astype(BF16)
+    bc = (mm(normed[...], w_bc_v[...]) * scale).astype(BF16)
     bc_s[...] = bc[:, : 2 * STATE]
     for f in range(2):
         for r in range(2):
@@ -150,10 +154,10 @@
     pl.semaphore_wait(barrier, TM - 1 + HT - 1)
 
     def bc_copy(to):
-        return remote(bct_send.at[to // GROUPS], bct.at[t], b_ssem.at[to], b_rsem.at[t], tm=to)
+        return remote(bct_send.at[to // GROUPS], bct.at[t], b_ssem.at[0], b_rsem.at[(to + t) % 2], tm=to)
 
     def bc_pass(source):
-        return remote(bct.at[source], bct.at[source], f_ssem.at[source], b_rsem.at[source], tm=t ^ 1)
+        return remote(bct.at[source], bct.at[source], b_ssem.at[1], b_rsem.at[1], tm=t ^ 1)
 
     @pl.loop(1, 4)
     def _(k):
@@ -163,7 +167,7 @@
     bct[t] = bct_send[own_row]
 
     def l_copy(to):
-        return remote(l_send.at[to % GROUPS, to // GROUPS], ltr.at[t], l_ssem.at[to], l_rsem.at[t], tm=to)
+        return remote(l_send.at[to % GROUPS, to // GROUPS], ltr.at[t], l_ssem.at[0], l_rsem.at[0], tm=to)
 
     def chunk_of(chunk):
         return pl.ds(pl.multiple_of(chunk * CHUNK_COLS, CHUNK_COLS), CHUNK_COLS)
@@ -172,7 +176,7 @@
         rows = pl.ds(pl.multiple_of((to // GROUPS) * COLS + chunk * CHUNK_COLS, CHUNK_COLS), CHUNK_COLS)
         return remote(
             x_all.at[:, rows, lanes_of(to % GROUPS)], xt.at[t, :, chunk_of(chunk)],
-            x_ssem.at[to], x_rsem.at[chunk, t], tm=to,
+            x_ssem.at[0], x_rsem.at[chunk], tm=to,
         )
 
     def owned(p):
@@ -185,12 +189,12 @@
         lanes = pl.ds(0, HALF + 128 * (1 - half))
         return remote(
             s_send.at[half, f, rows, lanes], s_recv.at[half, h, :, lanes],
-            s_ssem.at[to], s_rsem.at[half, h], height=to,
+            s_ssem.at[half], s_rsem.at[half], height=to,
         )
 
     def x_half(half):
         lanes = pl.ds(HALF * half, HALF)
-        xh = mm(normed[...], w_in_v[:, lanes]).astype(BF16)
+        xh = (mm(normed[...], w_in_v[:, lanes]) * scale).astype(BF16)
         x_all[0, :, lanes] = xh[:128]
         x_all[1, :, lanes] = xh[128:]
 
@@ -198,8 +202,10 @@
         load.wait()
     loads[2].wait()
     loads[3].wait()
-    x_half(0)
-    logits = mm_rows(normed[...], w_dt_v[...]).astype(BF16).astype(F32)
+    loads[4].wait()
+    for load in loads[5:]:
+        load.start()
+    logits = (mm_rows(normed[...], w_dt_v[...]) * scale).astype(BF16).astype(F32)
     dt = softplus(logits + dt_bias[...])
     rates = jnp.concatenate([rate[0:1, :], rate[1:2, :]], axis=1)
     decay = -dt * rates * LOG2E
@@ -247,9 +253,7 @@
         lanes = pl.ds(0, HALF + 128 * (1 - half))
         s_recv[half, h, :, lanes] = s_send[half, own_f, own_n, lanes]
 
-    loads[4].wait()
-    for load in loads[5:]:
-        load.start()
+    x_half(0)
     x_half(1)
 
     def x_send(chunk):
@@ -287,13 +291,15 @@
             @pl.when(k == 2 * step)
             def _():
                 loads[5 + step].wait()
-        v = mm(normed[...], w_in_v[:, pl.ds(pl.multiple_of(INNER + GL * k, 128), GL)]).astype(BF16).astype(F32)
+        v = mm(normed[...], w_in_v[:, pl.ds(pl.multiple_of(INNER + GL * k, 128), GL)])
+        v = (v * scale_in[...]).astype(BF16).astype(F32)
         gate[:, lanes_of(k)] = v / (1.0 + jnp.exp(-v))
+
+    received(bct.at[pl.ds(0, 3)], b_rsem.at[0])
 
     @pl.loop(1, 4)
     def _(k):
         source = (t + 2 * k) % TM
-        remote(bct_send.at[0], bct.at[source], b_ssem.at[source], b_rsem.at[source], tm=source).wait_recv()
         bc_pass(source).start()
 
     half = iota((128, 128), 1) < 64
@@ -329,19 +335,11 @@
     def i_copy(to, half):
         f, rows = owned(h)
         return remote(
-            inc_send.at[half, to], inc_recv.at[half, f, rows], i_ssem.at[to], i_rsem.at[half, h], height=to
+            inc_send.at[half, to], inc_recv.at[half, f, rows], i_ssem.at[half], i_rsem.at[half], height=to
         )
 
     def prefix(half):
-        @pl.loop(1, HT)
-        def _(k):
-            source = (h + k) % HT
-            lanes = pl.ds(0, HALF + 128 * (1 - half))
-            remote(
-                s_send.at[half, 0, pl.ds(0, 16), lanes], s_recv.at[half, source, :, lanes],
-                s_ssem.at[source], s_rsem.at[half, source], height=source,
-            ).wait_recv()
-
+        received(s_recv.at[half, pl.ds(0, HT - 1), :, pl.ds(0, HALF + 128 * (1 - half))], s_rsem.at[half])
         if half == 0:
             band_decays()
 
@@ -357,38 +355,24 @@
 
         inc_recv[half, own_f, own_n, :] = inc_send[half, h]
 
-    @pl.loop(1, TM)
-    def _(k):
-        source = (t + k) % TM
-        remote(l_send.at[0, 0], ltr.at[source], l_ssem.at[source], l_rsem.at[source], tm=source).wait_recv()
-
-    @pl.loop(0, 4)
-    def _(k):
-        source = (t + 2 * k) % TM ^ 1
-        remote(bct_send.at[0], bct.at[source], b_ssem.at[source], b_rsem.at[source], tm=source).wait_recv()
-
+    received(ltr.at[pl.ds(0, TM - 1)], l_rsem.at[0])
+    received(bct.at[pl.ds(0, 4)], b_rsem.at[1])
     columns = ltr[...].reshape(TM * 16, 128).T
     for s in range(TM):
         lcol[s] = columns[:, 16 * s : 16 * s + 16]
 
     state[...] = jnp.zeros_like(state)
 
-    def y_copy(to, cols, half):
+    def y_copy(to, cols, part):
         return remote(
-            y_send.at[to, :, cols], y_recv.at[t, :, cols], y_ssem.at[to], y_rsem.at[half, t], tm=to
+            y_send.at[to, :, cols], y_recv.at[t, :, cols], y_ssem.at[0], y_rsem.at[part], tm=to
         )
 
     @pl.loop(0, CHUNKS)
     def _(chunk):
         cols = chunk_of(chunk)
 
-        @pl.loop(1, TM)
-        def _(k):
-            source = (t + k) % TM
-            remote(
-                x_all.at[:, pl.ds(0, CHUNK_COLS), pl.ds(0, GL)], xt.at[source, :, cols],
-                x_ssem.at[source], x_rsem.at[chunk, source], tm=source,
-            ).wait_recv()
+        received(xt.at[pl.ds(0, TM - 1), :, cols], x_rsem.at[chunk])
 
         def tokens_of(f):
             return pl.ds(pl.multiple_of(f * COLS + chunk * CHUNK_COLS, CHUNK_COLS), CHUNK_COLS)
@@ -431,7 +415,7 @@
 
         @pl.loop(1, TM)
         def _(k):
-            y_copy((t + k) % TM, cols, chunk // 2).start()
+            y_copy((t + k) % TM, cols, chunk * 3 // 4).start()
 
         for half in range(2):
             @pl.when(chunk == half)
@@ -441,14 +425,7 @@
     y_recv[t] = y_send[t]
 
     for half in range(2):
-        @pl.loop(1, HT)
-        def _(k):
-            source = (h + k) % HT
-            f, rows = owned(source)
-            remote(
-                inc_send.at[half, source], inc_recv.at[half, f, rows],
-                i_ssem.at[source], i_rsem.at[half, source], height=source,
-            ).wait_recv()
+        received(inc_send.at[half, pl.ds(0, HT - 1)], i_rsem.at[half])
 
         for f in range(2):
             rows = slice(128 * f, 128 * f + 128)
@@ -457,72 +434,52 @@
                 earlier = mm(bc_s[rows, STATE:], inc_recv[half, f, :, pl.ds(GL * part, GL)])
                 sp_out[rows, lanes] += e_run[rows, lanes] * earlier
 
-    def out_copy(part, k):
-        rows = pl.ds(pl.multiple_of(k * COLS + part * 32, 32), 32)
-        return pltpu.make_async_copy(mixed_v.at[part, k], out.at[rows], out_sem.at[part, k])
-
-    @pl.loop(0, 2)
-    def _(part):
-        cols = pl.ds(pl.multiple_of(part * 32, 32), 32)
-
-        @pl.loop(1, TM)
-        def _(k):
-            source = (t + k) % TM
-            remote(
-                y_send.at[source, :, cols], y_recv.at[source, :, cols],
-                y_ssem.at[source], y_rsem.at[part, source], tm=source,
-            ).wait_recv()
-
+    def finish(part, start, width):
+        cols = pl.ds(start, width)
+
+        received(y_recv.at[pl.ds(0, TM - 1), :, cols], y_rsem.at[part])
+
+        scales = []
         for k in range(4):
             f, r = k // 2, k % 2
-            rows = pl.ds(pl.multiple_of(k * COLS + part * 32, 32), 32)
-            temporal = jnp.concatenate([y_recv[GROUPS * r + g, f, cols, :] for g in range(GROUPS)], axis=1)
-            gated = (sp_out[rows, :] + temporal.astype(F32)) * gate[rows, :]
-            mean_square = jnp.mean(gated * gated, axis=-1, keepdims=True)
-            normed[32 * k : 32 * k + 32, :] = (
-                gated * lax.rsqrt(mean_square + EPSILON) * out_gain[...].reshape(1, INNER)
-            ).astype(BF16)
-
-        @pl.when(part == 0)
-        def _():
-            loads[7].wait()
+            rows = slice(k * COLS + start, k * COLS + start + width)
+            squares = jnp.zeros((width, 128), F32)
+            for g in range(GROUPS):
+                y = y_recv[GROUPS * r + g, f, cols, :].astype(F32)
+                lanes = slice(GL * g, GL * g + GL)
+                gated = (sp_out[rows, lanes] + y) * gate[rows, lanes]
+                normed[width * k : width * k + width, lanes] = (
+                    gated * out_gain[GL * g : GL * g + GL].reshape(1, GL)
+                ).astype(BF16)
+                gated = gated * gated
+                squares += gated[:, :128] + gated[:, 128:256] + gated[:, 256:]
+            mean_square = jnp.sum(squares, axis=-1, keepdims=True) * (1.0 / INNER)
+            scales.append(lax.rsqrt(mean_square + EPSILON))
+        scale_v[0 : 4 * width, :] = jnp.concatenate(scales, axis=0)
 
         @pl.loop(0, 2)
         def _(k):
             lanes = pl.ds(pl.multiple_of(HALF * k, 128), HALF)
-            mixed = mm(normed[0:128, :], w_out_v[:, lanes]).astype(BF16)
+            mixed = mm(normed[0 : 4 * width, :], w_out_v[:, lanes]) * scale_v[0 : 4 * width, :]
+            mixed = mixed.astype(BF16)
             for block in range(4):
-                mixed_v[part, block, :, lanes] = mixed[32 * block : 32 * block + 32]
-
-        @pl.loop(0, 4)
-        def _(k):
-            out_copy(part, k).start()
-
-    @pl.loop(0, 4)
-    def _(k):
-        out_copy(0, k).wait()
-        out_copy(1, k).wait()
-
-    bc_copy(t ^ 1).wait_send()
-
-    @pl.loop(1, 4)
-    def _(k):
-        bc_copy((t + 2 * k) % TM).wait_send()
-        bc_pass((t + 2 * k) % TM).wait_send()
-
-    @pl.loop(1, TM)
-    def _(k):
-        to = (t + k) % TM
-        l_copy(to).wait_send()
-        remote(xt.at[to], xt.at[to], x_ssem.at[to], x_rsem.at[0, to], tm=to).wait_send()
-        y_copy(to, pl.ds(0, COLS), 0).wait_send()
-
-    @pl.loop(1, HT)
-    def _(k):
-        to = (h + k) % HT
-        for half in range(2):
-            s_copy(to, half).wait_send()
-            i_copy(to, half).wait_send()
+                out[block * COLS + start : block * COLS + start + width, lanes] = (
+                    mixed[width * block : width * block + width]
+                )
+
+    loads[7].wait()
+    finish(0, 0, 32)
+    finish(1, 32, 16)
+    finish(2, 48, 16)
+
+    sent(bct.at[pl.ds(0, 4)], b_ssem.at[0])
+    sent(bct.at[pl.ds(0, 3)], b_ssem.at[1])
+    sent(ltr.at[pl.ds(0, TM - 1)], l_ssem.at[0])
+    sent(xt.at[pl.ds(0, TM - 1)], x_ssem.at[0])
+    sent(y_send.at[pl.ds(0, TM - 1)], y_ssem.at[0])
+    for half in range(2):
+        sent(s_recv.at[half, pl.ds(0, HT - 1), :, pl.ds(0, HALF + 128 * (1 - half))], s_ssem.at[half])
+        sent(inc_send.at[half, pl.ds(0, HT - 1)], i_ssem.at[half])
 
 
 def per_device(tokens, norm_gain, in_weight, bc_weight, dt_weight, dt_bias, decay_rate, out_gain, out_weight):
@@ -572,14 +529,15 @@
             pltpu.VMEM((TM, 128, 16), F32),
             pltpu.VMEM((STATE, GL), F32),
             pltpu.VMEM((2, HT, HALF), F32),
-            pltpu.VMEM((2, 4, 32, D), BF16),
-            dma((8,)), dma((4,)), dma((2, 4)),
-            dma((TM,)), dma((CHUNKS, TM)),
-            dma((TM,)), dma((TM,)), dma((TM,)),
-            dma((TM,)), dma((TM,)),
-            dma((HT,)), dma((2, HT)),
-            dma((HT,)), dma((2, HT)),
-            dma((TM,)), dma((2, TM)),
+            pltpu.VMEM((128, 1), F32),
+            pltpu.VMEM((TOK, 1), F32),
+            dma((8,)), dma((4,)),
+            dma((1,)), dma((CHUNKS,)),
+            dma((2,)), dma((2,)),
+            dma((1,)), dma((1,)),
+            dma((2,)), dma((2,)),
+            dma((2,)), dma((2,)),
+            dma((1,)), dma((3,)),
         ],
         compiler_params=pltpu.CompilerParams(
             collective_id=0, has_side_effects=True, vmem_limit_bytes=40 * 1024 * 1024

time: 39.7 us -> 37 us (0.932)
  Pallas kernels: 38.7 us -> 35.9 us
    pallas_call x1, Pallas kernels: 38.7 us -> 35.9 us  [per_device(): pl.pallas_call(kernel, out_shape=jax.ShapeDtypeStruct((TOK, D), BF16), in...]
where the time goes in v5:
time: 37 us; the launch traced here: 36.8 us
  Pallas kernels  35.9 us (97%)
  local copies, waits for them, and re-layouts  0.88 us (2%)
    pallas_call x1, Pallas kernels, per_device(): pl.pallas_call(kernel, out_shape=jax.ShapeDtypeStruct((TOK, D), BF16), in...  35.9 us
    unnamed x1, local copies, waits for them, and re-layouts  0.88 us

profile of v5, /device:TPU:1, one launch (start us, length us, event | category | flops | bytes accessed | tf_op | source)
XLA Modules:
  0.0 36.8 jit_solution(3874579071423623009)
XLA Ops:
  0.0 35.9 %layer.1 = bf16[256,1536]{1,0:T(8,128)(2,1)S(1)} custom-call(bf16[256,1536]{1,0:T(8,128)(2,1)} %bitcast.5, f32[1536]{0:T(1024)} %gain_in.1, bf16[1536,3072]{1,0:T(8,128)(2,1)} %w_in.1, bf16[1536,512]{1,0:T(8,128)(2,1)} %w_bc.1, bf16[48,1536]{1,0:T(8,128)(2,1)} %bitcast.6, f32[1,48]{1,0:T(1,128)} %bitcast.7, f32[2,24]{1,0:T(2,128)} %rate_in.1, ...), custom_call_target="tpu_custom_call" | custom-call | tf_op jit(solution)/shard_map/layer/pallas_call | solution.py:491
  35.9 0.9 %copy.11 = bf16[2,2,64,1536]{3,2,1,0:T(8,128)(2,1)} copy(bf16[2,2,64,1536]{3,2,1,0:T(8,128)(2,1)S(1)} %bitcast.4) | data formatting | bytes 1572864

commit v6 on v5

--- a/solution.py
+++ b/solution.py
@@ -259,17 +259,17 @@
     def x_send(chunk):
         @pl.loop(1, TM)
         def _(k):
-            x_copy((t + k) % TM, chunk).start()
+            x_copy((t + 3 * k) % TM, chunk).start()
 
     x_send(0)
     state_half(0)
-    x_send(1)
+    state_half(1)
 
     @pl.loop(1, TM)
     def _(k):
         l_copy((t + k) % TM).start()
 
-    state_half(1)
+    x_send(1)
     x_send(2)
     x_send(3)
 
@@ -415,10 +415,10 @@
 
         @pl.loop(1, TM)
         def _(k):
-            y_copy((t + k) % TM, cols, chunk * 3 // 4).start()
+            y_copy((t + 3 * k) % TM, cols, chunk * 3 // 4).start()
 
         for half in range(2):
-            @pl.when(chunk == half)
+            @pl.when(chunk == 2 * half)
             def _():
                 prefix(half)
 

time: 37 us -> 35.8 us (0.968)
  Pallas kernels: 35.9 us -> 34.7 us
    pallas_call x1, Pallas kernels: 35.9 us -> 34.7 us  [per_device(): pl.pallas_call(kernel, out_shape=jax.ShapeDtypeStruct((TOK, D), BF16), in...]
where the time goes in v6:
time: 35.8 us; the launch traced here: 35.6 us
  Pallas kernels  34.7 us (97%)
  local copies, waits for them, and re-layouts  0.88 us (2%)
    pallas_call x1, Pallas kernels, per_device(): pl.pallas_call(kernel, out_shape=jax.ShapeDtypeStruct((TOK, D), BF16), in...  34.7 us
    unnamed x1, local copies, waits for them, and re-layouts  0.88 us

profile of v6, /device:TPU:1, one launch (start us, length us, event | category | flops | bytes accessed | tf_op | source)
XLA Modules:
  0.0 35.6 jit_solution(12973171032332286100)
XLA Ops:
  0.0 34.7 %layer.1 = bf16[256,1536]{1,0:T(8,128)(2,1)S(1)} custom-call(bf16[256,1536]{1,0:T(8,128)(2,1)} %bitcast.5, f32[1536]{0:T(1024)} %gain_in.1, bf16[1536,3072]{1,0:T(8,128)(2,1)} %w_in.1, bf16[1536,512]{1,0:T(8,128)(2,1)} %w_bc.1, bf16[48,1536]{1,0:T(8,128)(2,1)} %bitcast.6, f32[1,48]{1,0:T(1,128)} %bitcast.7, f32[2,24]{1,0:T(2,128)} %rate_in.1, ...), custom_call_target="tpu_custom_call" | custom-call | tf_op jit(solution)/shard_map/layer/pallas_call | solution.py:491
  34.7 0.9 %copy.11 = bf16[2,2,64,1536]{3,2,1,0:T(8,128)(2,1)} copy(bf16[2,2,64,1536]{3,2,1,0:T(8,128)(2,1)S(1)} %bitcast.4) | data formatting | bytes 1572864

commit v7 on v6

--- a/solution.py
+++ b/solution.py
@@ -67,10 +67,10 @@
     tokens, gain_in, w_in, w_bc, w_dt, dt_bias_in, rate_in, out_gain_in, w_out, out,
     gain, dt_bias, rate, out_gain,
     tok_v, w_in_v, w_bc_v, w_dt_v, w_out_v,
-    normed, x_all, gate, bc_s, bct_send, l_send, s_send,
-    xt, bct, ltr, s_recv, inc_send, inc_recv, y_send, y_recv,
+    normed, x_all, gate, bc_s, bct_send, l_send, d_send, s_send,
+    xt, bct, ltr, d_recv, s_recv, inc_send, inc_recv, y_send, y_recv,
     xd_s, sp_out, e_run, run_s, runt_s, spread_s, spread_t, order_t, lcol, state, d_exp,
-    scale_v, scale_in, load_sem, small_sem, x_ssem, x_rsem, b_ssem, b_rsem, l_ssem, l_rsem,
+    scale_v, scale_in, load_sem, small_sem, x_ssem, x_rsem, b_ssem, b_rsem, l_ssem, l_rsem, d_ssem, d_rsem,
     s_ssem, s_rsem, i_ssem, i_rsem, y_ssem, y_rsem,
 ):
     t = lax.axis_index("tm")
@@ -186,11 +186,12 @@
 
     def s_copy(to, half):
         f, rows = owned(to)
-        lanes = pl.ds(0, HALF + 128 * (1 - half))
         return remote(
-            s_send.at[half, f, rows, lanes], s_recv.at[half, h, :, lanes],
-            s_ssem.at[half], s_rsem.at[half], height=to,
+            s_send.at[half, f, rows], s_recv.at[half, h], s_ssem.at[half], s_rsem.at[half], height=to
         )
+
+    def d_copy(to):
+        return remote(d_send.at[to // 8], d_recv.at[h], d_ssem.at[0], d_rsem.at[0], height=to)
 
     def x_half(half):
         lanes = pl.ds(HALF * half, HALF)
@@ -202,9 +203,6 @@
         load.wait()
     loads[2].wait()
     loads[3].wait()
-    loads[4].wait()
-    for load in loads[5:]:
-        load.start()
     logits = (mm_rows(normed[...], w_dt_v[...]) * scale).astype(BF16).astype(F32)
     dt = softplus(logits + dt_bias[...])
     rates = jnp.concatenate([rate[0:1, :], rate[1:2, :]], axis=1)
@@ -227,8 +225,7 @@
         runt_s[f] = jnp.concatenate([run[128 * f : 128 * f + 128], jnp.zeros((128, 96), F32)], axis=1).T[:32]
     ends = [run[127:128], run[255:256]]
     for f in range(2):
-        total = jnp.concatenate([parts(jnp.exp2(ends[f]), 3).astype(F32), jnp.zeros((1, 32), F32)], axis=1)
-        s_send[0, f, :, HALF:] = jnp.broadcast_to(total, (STATE, 128)).astype(BF16)
+        d_send[f] = jnp.concatenate([jnp.exp2(ends[f]), jnp.zeros((1, 96), F32)], axis=1)
     end = jnp.concatenate([jnp.broadcast_to(e, (128, 32)) for e in ends], axis=0)
     to_end = parts(jnp.exp2(end - run) * dt_s, 2)
     dt_parts = parts(dt_s, 2)
@@ -250,10 +247,13 @@
         def _(k):
             s_copy((h + k) % HT, half).start()
 
-        lanes = pl.ds(0, HALF + 128 * (1 - half))
-        s_recv[half, h, :, lanes] = s_send[half, own_f, own_n, lanes]
+        s_recv[half, h] = s_send[half, own_f, own_n]
 
     x_half(0)
+    state_half(0)
+    loads[4].wait()
+    for load in loads[5:]:
+        load.start()
     x_half(1)
 
     def x_send(chunk):
@@ -262,7 +262,12 @@
             x_copy((t + 3 * k) % TM, chunk).start()
 
     x_send(0)
-    state_half(0)
+
+    @pl.loop(1, HT)
+    def _(k):
+        d_copy((h + k) % HT).start()
+
+    d_recv[h] = d_send[h // 8]
     state_half(1)
 
     @pl.loop(1, TM)
@@ -324,11 +329,8 @@
             sp_out[rows, lanes] = mm(jnp.concatenate(weights, axis=1), both_x)
 
     def band_decays():
-        row = iota((HT, 128), 0)
-        totals = jnp.zeros((HT, 128), F32)
-        for k in range(HT):
-            totals = jnp.where(row == k, s_recv[0, k, :, HALF:].astype(F32), totals)
-        totals = totals[:, :96].astype(BF16)
+        received(d_recv.at[pl.ds(0, HT - 1)], d_rsem.at[0])
+        totals = parts(jnp.concatenate([d_recv[k] for k in range(HT)], axis=0)[:, :32], 3)
         for half in range(2):
             d_exp[half] = mm(totals, spread_s[:, pl.ds(HALF * half, HALF)])
 
@@ -339,7 +341,7 @@
         )
 
     def prefix(half):
-        received(s_recv.at[half, pl.ds(0, HT - 1), :, pl.ds(0, HALF + 128 * (1 - half))], s_rsem.at[half])
+        received(s_recv.at[half, pl.ds(0, HT - 1)], s_rsem.at[half])
         if half == 0:
             band_decays()
 
@@ -347,7 +349,7 @@
         for k in range(HT):
             inc_send[half, k] = before.astype(BF16)
             if k < HT - 1:
-                before = before * d_exp[half, k : k + 1, :] + s_recv[half, k, :, :HALF].astype(F32)
+                before = before * d_exp[half, k : k + 1, :] + s_recv[half, k].astype(F32)
 
         @pl.loop(1, HT)
         def _(k):
@@ -415,7 +417,7 @@
 
         @pl.loop(1, TM)
         def _(k):
-            y_copy((t + 3 * k) % TM, cols, chunk * 3 // 4).start()
+            y_copy((t + 3 * k) % TM, cols, chunk // 2).start()
 
         for half in range(2):
             @pl.when(chunk == 2 * half)
@@ -469,16 +471,16 @@
 
     loads[7].wait()
     finish(0, 0, 32)
-    finish(1, 32, 16)
-    finish(2, 48, 16)
+    finish(1, 32, 32)
 
     sent(bct.at[pl.ds(0, 4)], b_ssem.at[0])
     sent(bct.at[pl.ds(0, 3)], b_ssem.at[1])
     sent(ltr.at[pl.ds(0, TM - 1)], l_ssem.at[0])
+    sent(d_recv.at[pl.ds(0, HT - 1)], d_ssem.at[0])
     sent(xt.at[pl.ds(0, TM - 1)], x_ssem.at[0])
     sent(y_send.at[pl.ds(0, TM - 1)], y_ssem.at[0])
     for half in range(2):
-        sent(s_recv.at[half, pl.ds(0, HT - 1), :, pl.ds(0, HALF + 128 * (1 - half))], s_ssem.at[half])
+        sent(s_recv.at[half, pl.ds(0, HT - 1)], s_ssem.at[half])
         sent(inc_send.at[half, pl.ds(0, HT - 1)], i_ssem.at[half])
 
 
@@ -509,11 +511,13 @@
             pltpu.VMEM((TOK, 2 * STATE), BF16),
             pltpu.VMEM((2, 2, COLS, 2 * STATE), BF16),
             pltpu.VMEM((GROUPS, 2, 16, 128), F32),
-            pltpu.VMEM((2, 2, STATE, HALF + 128), BF16),
+            pltpu.VMEM((2, 1, 128), F32),
+            pltpu.VMEM((2, 2, STATE, HALF), BF16),
             pltpu.VMEM((TM, 2, COLS, GL), BF16),
             pltpu.VMEM((TM, 2, COLS, 2 * STATE), BF16),
             pltpu.VMEM((TM, 16, 128), F32),
-            pltpu.VMEM((2, HT, 16, HALF + 128), BF16),
+            pltpu.VMEM((HT, 1, 128), F32),
+            pltpu.VMEM((2, HT, 16, HALF), BF16),
             pltpu.VMEM((2, HT, 16, HALF), BF16),
             pltpu.VMEM((2, 2, STATE, HALF), BF16),
             pltpu.VMEM((TM, 2, COLS, GL), BF16),
@@ -535,9 +539,10 @@
             dma((1,)), dma((CHUNKS,)),
             dma((2,)), dma((2,)),
             dma((1,)), dma((1,)),
+            dma((1,)), dma((1,)),
             dma((2,)), dma((2,)),
             dma((2,)), dma((2,)),
-            dma((1,)), dma((3,)),
+            dma((1,)), dma((2,)),
         ],
         compiler_params=pltpu.CompilerParams(
             collective_id=0, has_side_effects=True, vmem_limit_bytes=40 * 1024 * 1024

time: 35.8 us -> 34.5 us (0.964)
  Pallas kernels: 34.7 us -> 33.5 us
    pallas_call x1, Pallas kernels: 34.7 us -> 33.5 us  [per_device(): pl.pallas_call(kernel, out_shape=jax.ShapeDtypeStruct((TOK, D), BF16), in...]
where the time goes in v7:
time: 34.5 us; the launch traced here: 34.4 us
  Pallas kernels  33.5 us (97%)
  local copies, waits for them, and re-layouts  0.88 us (3%)
    pallas_call x1, Pallas kernels, per_device(): pl.pallas_call(kernel, out_shape=jax.ShapeDtypeStruct((TOK, D), BF16), in...  33.5 us
    unnamed x1, local copies, waits for them, and re-layouts  0.88 us

profile of v7, /device:TPU:1, one launch (start us, length us, event | category | flops | bytes accessed | tf_op | source)
XLA Modules:
  0.0 34.4 jit_solution(14673977330264651439)
XLA Ops:
  0.0 33.5 %layer.1 = bf16[256,1536]{1,0:T(8,128)(2,1)S(1)} custom-call(bf16[256,1536]{1,0:T(8,128)(2,1)} %bitcast.5, f32[1536]{0:T(1024)} %gain_in.1, bf16[1536,3072]{1,0:T(8,128)(2,1)} %w_in.1, bf16[1536,512]{1,0:T(8,128)(2,1)} %w_bc.1, bf16[48,1536]{1,0:T(8,128)(2,1)} %bitcast.6, f32[1,48]{1,0:T(1,128)} %bitcast.7, f32[2,24]{1,0:T(2,128)} %rate_in.1, ...), custom_call_target="tpu_custom_call" | custom-call | tf_op jit(solution)/shard_map/layer/pallas_call | solution.py:493
  33.5 0.9 %copy.11 = bf16[2,2,64,1536]{3,2,1,0:T(8,128)(2,1)} copy(bf16[2,2,64,1536]{3,2,1,0:T(8,128)(2,1)S(1)} %bitcast.4) | data formatting | bytes 1572864

commit v8 on v7

--- a/solution.py
+++ b/solution.py
@@ -459,9 +459,8 @@
             scales.append(lax.rsqrt(mean_square + EPSILON))
         scale_v[0 : 4 * width, :] = jnp.concatenate(scales, axis=0)
 
-        @pl.loop(0, 2)
-        def _(k):
-            lanes = pl.ds(pl.multiple_of(HALF * k, 128), HALF)
+        for k in range(2):
+            lanes = pl.ds(HALF * k, HALF)
             mixed = mm(normed[0 : 4 * width, :], w_out_v[:, lanes]) * scale_v[0 : 4 * width, :]
             mixed = mixed.astype(BF16)
             for block in range(4):

time: 34.5 us -> 34.1 us (0.988)
  Pallas kernels: 33.5 us -> 33.1 us
    pallas_call x1, Pallas kernels: 33.5 us -> 33.1 us  [per_device(): pl.pallas_call(kernel, out_shape=jax.ShapeDtypeStruct((TOK, D), BF16), in...]
where the time goes in v8:
time: 34.1 us; the launch traced here: 34 us
  Pallas kernels  33.1 us (97%)
  local copies, waits for them, and re-layouts  0.88 us (3%)
    pallas_call x1, Pallas kernels, per_device(): pl.pallas_call(kernel, out_shape=jax.ShapeDtypeStruct((TOK, D), BF16), in...  33.1 us
    unnamed x1, local copies, waits for them, and re-layouts  0.88 us

profile of v8, /device:TPU:1, one launch (start us, length us, event | category | flops | bytes accessed | tf_op | source)
XLA Modules:
  0.0 34.0 jit_solution(7875047939095165690)
XLA Ops:
  0.0 33.1 %layer.1 = bf16[256,1536]{1,0:T(8,128)(2,1)S(1)} custom-call(bf16[256,1536]{1,0:T(8,128)(2,1)} %bitcast.5, f32[1536]{0:T(1024)} %gain_in.1, bf16[1536,3072]{1,0:T(8,128)(2,1)} %w_in.1, bf16[1536,512]{1,0:T(8,128)(2,1)} %w_bc.1, bf16[48,1536]{1,0:T(8,128)(2,1)} %bitcast.6, f32[1,48]{1,0:T(1,128)} %bitcast.7, f32[2,24]{1,0:T(2,128)} %rate_in.1, ...), custom_call_target="tpu_custom_call" | custom-call | tf_op jit(solution)/shard_map/layer/pallas_call | solution.py:492
  33.1 0.9 %copy.11 = bf16[2,2,64,1536]{3,2,1,0:T(8,128)(2,1)} copy(bf16[2,2,64,1536]{3,2,1,0:T(8,128)(2,1)S(1)} %bitcast.4) | data formatting | bytes 1572864
